TPU v7x, 32 devices: a whole 2x2x4 slice. The times are simulated.
32 devices in a mesh: frame: 4 (over y, core), space: 8 (over z, x).
Axes of the slice: x: 2, y: 2, z: 4, core: 2. Of those that a mesh axis runs over, the one named last changes fastest.
Arguments:
- frames_in: bfloat16 [8, 1024, 2048], P('frame', 'space'), may hold values from -6 to 6
- levels: int32 [8], P('frame'), may hold values from 1 to 899
- fresh: bfloat16 [1024, 2048], P('space'), may hold values from -6 to 6
- w_mod: bfloat16 [256, 4096], replicated, may hold values from -0.375 to 0.375
- w_qkv: bfloat16 [2048, 3072], P('space'), may hold values from -0.26516504 to 0.26516504
- q_gain: float32 [8], replicated, may hold values from 0.5 to 64
- w_out: bfloat16 [1024, 2048], P('space'), may hold values from -0.1875 to 0.1875
Outputs:
- frames_out: bfloat16 [8, 1024, 2048], P('frame', 'space')
All inputs are finite; a program needn't handle non-finite values.
Results may differ from a plain program's by a relative error of at most 0.0075.
The roundings to bfloat16 on the way count: a program that leaves them out, or rounds other values in their place, can miss the bound.
Values may be sent and summed in bfloat16 or wider, within the bound.
A program may use at most 128 MiB of HBM per device.

v0:
```python
import math

import jax
import jax.numpy as jnp
from jax import lax
from jax.sharding import PartitionSpec as P

LEVELS = 1000
FRAMES = 8


def with_halo(cells, sides, width):
    for axis, dim in sides:
        count = lax.axis_size(axis)
        head = lax.slice_in_dim(cells, 0, width, axis=dim)
        tail = lax.slice_in_dim(cells, cells.shape[dim] - width, cells.shape[dim], axis=dim)
        cells = jnp.concatenate(
            [
                lax.ppermute(tail, axis, [(i, (i + 1) % count) for i in range(count)]),
                cells,
                lax.ppermute(head, axis, [((i + 1) % count, i) for i in range(count)]),
            ],
            axis=dim,
        )
    return cells


def from_behind(array, axis, by):
    count = lax.axis_size(axis)
    pairs = [(i, i + by) for i in range(count) if 0 <= i + by < count]
    return lax.ppermute(array, axis, pairs)


def embed(levels, freq_count):
    half = freq_count // 2
    freqs = jnp.exp(-math.log(10000.0) * jnp.arange(half, dtype=jnp.float32) / half)
    angles = levels.astype(jnp.float32)[:, None] * freqs[None, :]
    return jnp.concatenate([jnp.cos(angles), jnp.sin(angles)], axis=1).astype(jnp.bfloat16)


def alpha_bar(steps):
    frac = steps.astype(jnp.float32) / LEVELS
    return jnp.cos((frac + 0.008) / 1.008 * (math.pi / 2)) ** 2


def body(frames_in, levels, fresh, w_mod, w_qkv, q_gain, w_out):
    local_frames, rows, width = frames_in.shape
    heads = q_gain.shape[0]
    head_dim = w_qkv.shape[1] // (3 * heads)
    inv = 1.0 / math.sqrt(head_dim)
    mod = jnp.dot(embed(levels, w_mod.shape[0]), w_mod, preferred_element_type=jnp.float32)
    shift = mod[:, :width]
    scale = mod[:, width:]
    x32 = frames_in.astype(jnp.float32)
    mean = jnp.mean(x32, axis=-1, keepdims=True)
    var = jnp.mean((x32 - mean) ** 2, axis=-1, keepdims=True)
    normed = (x32 - mean) * lax.rsqrt(var + 1e-06)
    xm = (normed * (1.0 + scale[:, None, :]) + shift[:, None, :]).astype(jnp.bfloat16)
    xm = xm.reshape(local_frames * rows, width)
    columns = xm
    qkv = jnp.dot(
        columns,
        lax.all_gather(w_qkv, "space", axis=0, tiled=True),
        preferred_element_type=jnp.float32,
    )
    qkv = qkv.reshape(local_frames, rows, 3, heads, head_dim)
    query = qkv[:, :, 0]
    key = qkv[:, :, 1]
    query = (
        query
        * lax.rsqrt(jnp.mean(query * query, axis=-1, keepdims=True) + 1e-06)
        * q_gain[None, None, :, None]
    )
    key = key * lax.rsqrt(jnp.mean(key * key, axis=-1, keepdims=True) + 1e-06)
    q_norm = query.astype(jnp.bfloat16)
    k_norm = key.astype(jnp.bfloat16)
    v_vals = qkv[:, :, 2].astype(jnp.bfloat16)
    stacked = jnp.stack([k_norm, v_vals], axis=0)
    padded = with_halo(stacked, (("space", 2),), rows)
    spatial = (
        jnp.einsum("frhd,fkhd->fhrk", q_norm, padded[0], preferred_element_type=jnp.float32) * inv
    )
    kk = jnp.arange(3 * rows)[None, :]
    rr = jnp.arange(rows)[:, None]
    band = jnp.abs(kk - rr - rows) <= rows
    spatial = jnp.where(band[None, None], spatial, -1e30)
    top_space = jnp.max(spatial, axis=-1)
    p_space = jnp.where(band[None, None], jnp.exp(spatial - top_space[..., None]), 0.0)
    sum_space = jnp.sum(p_space, axis=-1).transpose(0, 2, 1)
    acc_space = jnp.einsum(
        "fhrk,fkhd->frhd",
        p_space.astype(jnp.bfloat16),
        padded[1],
        preferred_element_type=jnp.float32,
    )
    top_space = top_space.transpose(0, 2, 1)
    mine = lax.axis_index("frame") * local_frames + jnp.arange(local_frames)
    start_top = jnp.full((local_frames, rows, heads), -1e30, jnp.float32)
    k_piece = lax.all_gather(k_norm, "frame", axis=0, tiled=True)
    other = jnp.arange(k_piece.shape[0])
    causal = jnp.logical_and(other[None, :] < mine[:, None], True)[:, None, None, :]
    scores = (
        jnp.einsum("frhd,grhd->frhg", q_norm, k_piece, preferred_element_type=jnp.float32) * inv
    )
    scores = jnp.where(causal, scores, -1e30)
    top_new = jnp.maximum(start_top, jnp.max(scores, axis=-1))
    probs = jnp.where(causal, jnp.exp(scores - top_new[..., None]), 0.0)
    sums = jnp.sum(probs, axis=-1)
    acc = jnp.einsum(
        "frhg,grhd->frhd",
        probs.astype(jnp.bfloat16),
        lax.all_gather(v_vals, "frame", axis=0, tiled=True),
        preferred_element_type=jnp.float32,
    )
    acc_time = acc
    top_all = jnp.maximum(top_space, top_new)
    weight_space = jnp.exp(top_space - top_all)
    weight_time = jnp.exp(top_new - top_all)
    total = sum_space * weight_space + sums * weight_time
    acc = acc_space * weight_space[..., None] + acc_time * weight_time[..., None]
    attended = (
        (acc / total[..., None]).astype(jnp.bfloat16).reshape(local_frames * rows, heads * head_dim)
    )
    columns = attended
    projected = jnp.dot(
        columns,
        lax.all_gather(w_out, "space", axis=0, tiled=True),
        preferred_element_type=jnp.float32,
    )
    eps = x32 + projected.reshape(local_frames, rows, width)
    later = jnp.maximum(levels - LEVELS // FRAMES, 0)
    a_now = alpha_bar(levels)[:, None, None]
    a_later = alpha_bar(later)[:, None, None]
    clean = (x32 - jnp.sqrt(1.0 - a_now) * eps) / jnp.sqrt(a_now)
    denoised = (jnp.sqrt(a_later) * clean + jnp.sqrt(1.0 - a_later) * eps).astype(jnp.bfloat16)
    arriving = from_behind(denoised[0:1], "frame", -1)
    is_last = lax.axis_index("frame") == lax.axis_size("frame") - 1
    tail = jnp.where(is_last, fresh[None], arriving)
    return jnp.concatenate([denoised[1:], tail], axis=0)


def solution(mesh):
    return jax.shard_map(
        body,
        mesh=mesh,
        in_specs=(
            P("frame", "space", None),
            P("frame"),
            P("space", None),
            P(),
            P("space", None),
            P(),
            P("space", None),
        ),
        out_specs=P("frame", "space", None),
        check_vma=False,
    )
```

profile of v0, /device:TPU:1, one launch (start us, length us, event | category | flops | bytes accessed | tf_op | source)
XLA Modules:
  0.0 359.7 jit_solution(436228587880046304)
XLA Ops:
  8.0 1.4 convert_reduce_fusion
  10.4 177.3 %all-gather.6.cloned.1.call-done = bf16[2048,3072]{1,0:T(8,128)(2,1)} async-done(((bf16[256,3072]{1,0:T(8,128)(2,1)}), bf16[2048,3072]{1,0:T(8,128)(2,1)}) %all-gather.6.cloned.1.call-update) | async-done | bytes 12582928 | tf_op jit(solution)/shard_map/all_gather | solution.py:63
  187.7 15.6 %copy.33 = bf16[3072,2048]{1,0:T(8,128)(2,1)} copy(bf16[3072,2048]{0,1:T(8,128)(2,1)} %bitcast.92) | data formatting | bytes 25165824 | tf_op jit(solution)/shard_map/dot_general | solution.py:61
  203.3 7.3 %fusion.51 = f32[2,128,3,8,128]{1,4,3,2,0:T(8,128)S(1)} fusion(bf16[3,8,128,2048,1]{3,2,1,0,4:T(8,128)(2,1)} %bitcast.93, bf16[2,128,2048]{2,1,0:T(8,128)(2,1)S(1)} %copy-done.5, f32[2,2048]{1,0:T(2,128)S(1)} %get-tuple-element.17, f32[2,2048]{1,0:T(2,128)S(1)} %get-tuple-element.16, f32[2,128]{1,0:T(2,128)S(1)} %add_rsqrt_fusion.2, ...), kind=kOutput, calls=%fused_computation.43 | convolution fusion | flops 3224371200 | bytes 16812032 | tf_op jit(solution)/shard_map/dot_general | solution.py:61
  210.8 1.5 copy-done.1
  214.6 1.3 slice.67
  217.6 1.3 slice_bitcast_fusion.13
  218.9 1.4 fusion.55
  221.4 1.6 collective-permute-start.1
  223.2 2.0 copy.39
  225.2 42.4 %collective-permute-done.1 = bf16[2,2,128,8,128]{2,4,3,1,0:T(8,128)(2,1)} collective-permute-done((bf16[2,2,128,8,128]{2,4,3,1,0:T(8,128)(2,1)}, bf16[2,2,128,8,128]{2,4,3,1,0:T(8,128)(2,1)}, u32[]{:S(2)}, u32[]{:S(2)}) %collective-permute-start.1) | collective-permute-done | bytes 1048608 | tf_op jit(solution)/shard_map/ppermute | solution.py:21
  268.2 1.8 pad_maximum_fusion
  270.0 1.7 copy-done.3
  272.5 1.7 copy-done.2
  274.2 1.1 fusion.7
  275.4 5.0 %fusion.83 = (f32[2,128,8]{0,2,1:T(8,128)S(1)}, f32[2,128,8,8]{3,0,2,1:T(2,128)}) fusion(bf16[2,128,8,128]{3,0,2,1:T(2,128)(2,1)S(1)} %copy-done.7, bf16[8,128,8,128]{3,2,1,0:T(8,128)(2,1)} %all-gather.8.cloned.1.call-done, pred[2,8]{1,0:T(4,128)(4,1)S(1)} %iota_compare_fusion), kind=kOutput, calls=%fused_computation.102 | convolution fusion | flops 4241408 | bytes 2695184 | tf_op jit(solution)/shard_map/frhd,grhd->frhg/dot_general | solution.py:103
  280.9 5.2 %fusion.16 = f32[128,8,128,2]{2,3,1,0:T(2,128)} fusion(bf16[8,128,1,8,128]{4,3,2,1,0:T(8,128)(2,1)} %all-gather.12.cloned.1.call-done, f32[2,128,8,8]{3,0,2,1:T(2,128)} %get-tuple-element.25, pred[2,8]{1,0:T(4,128)(4,1)S(1)} %iota_compare_fusion, f32[2,128,8]{0,2,1:T(8,128)S(1)} %copy.43), kind=kOutput, calls=%fused_computation.21 | convolution fusion | flops 4243456 | bytes 3219472 | tf_op jit(solution)/shard_map/frhg,grhd->frhd/dot_general | solution.py:109
  286.1 2.3 copy.44
  288.4 3.8 %fusion.63 = f32[2,128,8]{0,2,1:T(8,128)S(1)} fusion(f32[2,128,8,8]{3,0,2,1:T(2,128)} %get-tuple-element.25, f32[2,128,8]{0,2,1:T(8,128)S(1)} %copy.43, pred[2,8]{1,0:T(4,128)(4,1)S(1)} %iota_compare_fusion), kind=kLoop, calls=%fused_computation.66 | loop fusion | flops 47104 | bytes 81936 | tf_op jit(solution)/shard_map/reduce_sum | solution.py:108
  292.5 4.6 %divide_convert_fusion = bf16[2,128,8,128]{1,3,2,0:T(8,128)(2,1)} fusion(f32[128,8,128,2]{0,2,1,3:T(8,128)} %copy.44, f32[2,8,128,384]{3,2,1,0:T(8,128)} %copy-done.2, f32[2,8,128]{2,1,0:T(8,128)S(1)} %get-tuple-element.26, pred[128,384]{1,0:T(8,128)(4,1)S(1)} %abs_compare_fusion, bf16[2,2,384,8,128]{2,4,3,1,0:T(8,128)(2,1)} %copy-done.3, ...), kind=kOutput, calls=%fused_computation.55 | convolution fusion | flops 206569472 | bytes 6373376 | tf_op jit(solution)/shard_map/fhrk,fkhd->frhd/dot_general | solution.py:90
  297.1 37.2 %all-gather.10.cloned.1.call-done = bf16[1024,2048]{1,0:T(8,128)(2,1)} async-done(((bf16[128,2048]{1,0:T(8,128)(2,1)}), bf16[1024,2048]{1,0:T(8,128)(2,1)}) %all-gather.10.cloned.1.call-update) | async-done | bytes 4194320 | tf_op jit(solution)/shard_map/all_gather | solution.py:127
  334.3 4.0 %fusion.21 = bf16[2,128,2048]{2,1,0:T(8,128)(2,1)S(1)} fusion(bf16[2,128,2048]{2,1,0:T(8,128)(2,1)S(1)} %copy-done.6, bf16[2,128,1024]{1,2,0:T(8,128)(2,1)} %bitcast.94, bf16[1024,2048]{1,0:T(8,128)(2,1)} %all-gather.10.cloned.1.call-done, f32[2]{0:T(128)S(1)} %subtract_sqrt_fusion, f32[2]{0:T(128)S(1)} %get-tuple-element.21, f32[2]{0:T(128)S(1)} %get-tuple-element.20, ...), kind=kOutput, calls=%fused_computation.26 | convolution fusion | flops 1078460416 | bytes 6815776 | tf_op jit(solution)/shard_map/dot_general | solution.py:125
  339.1 3.8 %collective-permute-start.2 = (bf16[1,128,2048]{2,1,0:T(8,128)(2,1)}, bf16[1,128,2048]{2,1,0:T(8,128)(2,1)S(1)}, u32[]{:S(2)}, u32[]{:S(2)}) collective-permute-start(bf16[1,128,2048]{2,1,0:T(8,128)(2,1)} %get-tuple-element.15), channel_id=1, source_target_pairs={{8,0},{16,8},{24,16},{9,1},{17,9},{25,17},{10,2},{18,10},{26,18},{... | collective-permute-start | bytes 1572872 | tf_op jit(solution)/shard_map/ppermute | solution.py:31
  342.9 8.1 %collective-permute-done.2 = bf16[1,128,2048]{2,1,0:T(8,128)(2,1)S(1)} collective-permute-done((bf16[1,128,2048]{2,1,0:T(8,128)(2,1)}, bf16[1,128,2048]{2,1,0:T(8,128)(2,1)S(1)}, u32[]{:S(2)}, u32[]{:S(2)}) %collective-permute-start.2) | collective-permute-done | bytes 524320 | tf_op jit(solution)/shard_map/ppermute | solution.py:31
  (57 shorter events, 12.9 us)
Async XLA Ops:
  6.5 3.5 copy-start
  6.5 2.9 copy-start.5
  6.5 181.1 %all-gather.6.cloned.1.call-start = ((), (), s32[]{:S(2)}) async-start(), calls=%async_computation | async-start | bytes 14155776 | tf_op jit(solution)/shard_map/all_gather | solution.py:63
  7.3 268.1 %all-gather.8.cloned.1.call-start = ((), (), s32[]{:S(2)}) async-start(), calls=%async_computation.1 | async-start | bytes 2621440 | tf_op jit(solution)/shard_map/all_gather | solution.py:99
  203.3 8.9 %copy-start.9 = (f32[8]{0:T(128)S(1)}, f32[8]{0:T(128)}, u32[]{:S(2)}) copy-start(f32[8]{0:T(128)} %param.12) | copy-start | bytes 100
  210.6 1.7 copy-start.1
  214.5 66.4 %all-gather.12.cloned.1.call-start = ((), (), s32[]{:S(2)}) async-start(), calls=%async_computation.3 | async-start | bytes 2621440 | tf_op jit(solution)/shard_map/all_gather | solution.py:112
  217.0 6.2 %copy-start.8 = (s32[2]{0:T(128)S(1)}, s32[2]{0:T(128)}, u32[]{:S(2)}) copy-start(s32[2]{0:T(128)} %param.8) | copy-start | bytes 28
  217.0 117.3 %all-gather.10.cloned.1.call-start = ((), (), s32[]{:S(2)}) async-start(), calls=%async_computation.2 | async-start | bytes 4718592 | tf_op jit(solution)/shard_map/all_gather | solution.py:127
  221.4 46.3 %collective-permute-start.1 = (bf16[2,2,128,8,128]{2,4,3,1,0:T(8,128)(2,1)}, bf16[2,2,128,8,128]{2,4,3,1,0:T(8,128)(2,1)}, u32[]{:S(2)}, u32[]{:S(2)}) collective-permute-start(bf16[2,2,128,8,128]{2,4,3,1,0:T(8,128)(2,1)} %pad_maximum_fusion.1), channel_id=1, source_target_pairs={{1,0},{2,1},{3,2},{4,3},{5,4},{6,5},{7,6},{0,7},{9,8},{10,9},{11,1... | collective-permute-start | bytes 3145736 | tf_op jit(solution)/shard_map/ppermute | solution.py:21
  223.0 45.2 %collective-permute-start = (bf16[2,2,128,8,128]{2,4,3,1,0:T(8,128)(2,1)}, bf16[2,2,128,8,128]{2,4,3,1,0:T(8,128)(2,1)}, u32[]{:S(2)}, u32[]{:S(2)}) collective-permute-start(bf16[2,2,128,8,128]{2,4,3,1,0:T(8,128)(2,1)} %pad_maximum_fusion.1), channel_id=1, source_target_pairs={{0,1},{1,2},{2,3},{3,4},{4,5},{5,6},{6,7},{7,0},{8,9},{9,10},{10,1... | collective-permute-start | bytes 3145736 | tf_op jit(solution)/shard_map/ppermute | solution.py:19
  225.2 46.5 %copy-start.4 = (bf16[2,128,8,128]{1,3,2,0:T(8,128)(2,1)S(1)}, bf16[2,128,8,128]{1,3,2,0:T(8,128)(2,1)}, u32[]{:S(2)}) copy-start(bf16[2,128,8,128]{1,3,2,0:T(8,128)(2,1)} %get-tuple-element.13) | copy-start | bytes 1572868
  270.0 1.7 copy-start.3
  271.7 3.7 %copy-start.7 = (bf16[2,128,8,128]{3,0,2,1:T(2,128)(2,1)S(1)}, bf16[2,128,8,128]{3,0,2,1:T(2,128)(2,1)}, u32[]{:S(2)}) copy-start(bf16[2,128,8,128]{3,0,2,1:T(2,128)(2,1)} %copy.39) | copy-start | bytes 1572868
  272.5 1.7 copy-start.2
  292.4 41.8 %copy-start.6 = (bf16[2,128,2048]{2,1,0:T(8,128)(2,1)S(1)}, bf16[2,128,2048]{2,1,0:T(8,128)(2,1)}, u32[]{:S(2)}) copy-start(bf16[2,128,2048]{2,1,0:T(8,128)(2,1)} %param.7) | copy-start | bytes 3145732
  339.1 11.9 %collective-permute-start.2 = (bf16[1,128,2048]{2,1,0:T(8,128)(2,1)}, bf16[1,128,2048]{2,1,0:T(8,128)(2,1)S(1)}, u32[]{:S(2)}, u32[]{:S(2)}) collective-permute-start(bf16[1,128,2048]{2,1,0:T(8,128)(2,1)} %get-tuple-element.15), channel_id=1, source_target_pairs={{8,0},{16,8},{24,16},{9,1},{17,9},{25,17},{10,2},{18,10},{26,18},{... | collective-permute-start | bytes 1572872 | tf_op jit(solution)/shard_map/ppermute | solution.py:31
Sparse Core Ops, SparseCore 0:
  9.6 178.0 all-gather.5
  214.6 21.5 all-gather.7
  237.8 22.5 all-gather.11
  262.4 71.7 all-gather.9
where the time goes:
time: 361 us; the launch traced here: 360 us
  waiting for transfers between devices  267 us (74%)
  local copies, waits for them, and re-layouts  31.2 us (9%)
  matrix products  27.2 us (8%)
  other arithmetic  15.6 us (4%)
  between operations  13.4 us (4%)
  starting transfers between devices  5.48 us (2%)
    all_gather x1, waiting for transfers between devices, body(): lax.all_gather(w_qkv, 'space', axis=0, tiled=True)  177 us
    ppermute x1, waiting for transfers between devices, with_halo(): lax.ppermute(head, axis, [((i + 1) % count, i) for i in range(count)])  42.4 us
    all_gather x1, waiting for transfers between devices, body(): lax.all_gather(w_out, 'space', axis=0, tiled=True)  37.2 us
    dot_general x1, local copies, waits for them, and re-layouts, body(): jnp.dot(columns, lax.all_gather(w_qkv, 'space', axis=0, tiled=True), pref...  15.6 us
    ppermute x1, waiting for transfers between devices, from_behind(): return lax.ppermute(array, axis, pairs)  8.14 us
    dot_general x1, matrix products, body(): jnp.dot(columns, lax.all_gather(w_qkv, 'space', axis=0, tiled=True), pref...  7.25 us
  transfers between devices with their start and end apart: 7, of which 5 were waited for; matrix products, arithmetic and copies ran while one was open for 10% of the time, Pallas kernels for 0%

commit v1 on v0

v1 whole, which is shorter than its diff:
```python
import functools
import math

import jax
import jax.numpy as jnp
from jax import lax
from jax.experimental import pallas as pl
from jax.experimental.pallas import tpu as pltpu
from jax.sharding import PartitionSpec as P

LEVELS = 1000
FRAMES = 8
MESH = pl.DeviceIdType.MESH
VMEM_LIMIT = 56 * 1024 * 1024


def from_behind(array, axis, by):
    count = lax.axis_size(axis)
    pairs = [(i, i + by) for i in range(count) if 0 <= i + by < count]
    return lax.ppermute(array, axis, pairs)


def embed(levels, freq_count):
    half = freq_count // 2
    freqs = jnp.exp(-math.log(10000.0) * jnp.arange(half, dtype=jnp.float32) / half)
    angles = levels.astype(jnp.float32)[:, None] * freqs[None, :]
    return jnp.concatenate([jnp.cos(angles), jnp.sin(angles)], axis=1).astype(jnp.bfloat16)


def alpha_bar(steps):
    frac = steps.astype(jnp.float32) / LEVELS
    return jnp.cos((frac + 0.008) / 1.008 * (math.pi / 2)) ** 2


class Place:
    def __init__(self, space):
        self.space = space
        self.pairs = space // 2
        self.f = lax.axis_index("frame")
        self.s = lax.axis_index("space")
        self.pair = self.s // 2
        self.side = self.s % 2
        core = self.f % 2
        self.f_core = self.f + 1 - 2 * core
        self.f_far = (self.f + 2) % 4
        self.f_diag = (self.f_core + 2) % 4
        self.s_side = self.s + 1 - 2 * self.side

    def pair_at(self, k):
        return lax.rem(self.pair + k, self.pairs)

    def shard_at(self, q):
        return 2 * self.pair_at(q // 2) + lax.rem(self.side + q, 2)


def remote(src, dst, send_sem, recv_sem, device):
    return pltpu.make_async_remote_copy(
        src_ref=src,
        dst_ref=dst,
        send_sem=send_sem,
        recv_sem=recv_sem,
        device_id=device,
        device_id_type=MESH,
    )


def greet(at):
    barrier = pltpu.get_barrier_semaphore()

    def hello(f, s):
        pl.semaphore_signal(barrier, inc=1, device_id=(f, s), device_id_type=MESH)

    for k in range(1, at.pairs):
        hello(at.f, 2 * at.pair_at(k) + at.side)
    hello(at.f, at.s_side)
    hello(at.f_far, at.s)
    hello(at.f_core, at.s)
    pl.semaphore_wait(barrier, at.pairs + 2)


def qkv_kernel(
    space, gain_ref, xm_ref, w_ref, q_ref, kv_ref, xg, wg,
    local_sem, xm_send, xm_recv, send_a, send_r, send_x, send_y, send_c, send_d, recv,
):
    at = Place(space)
    rows = xm_ref.shape[0]
    heads = wg.shape[0]
    frames = q_ref.shape[0]
    block = rows // frames
    hd = q_ref.shape[3]
    f, s, side = at.f, at.s, at.side
    greet(at)

    def direct(k):
        return remote(
            w_ref.at[heads * side + f], wg.at[f, s], send_a.at[k], recv.at[f, s],
            (f, 2 * at.pair_at(k) + side),
        )

    def relay(k):
        return remote(
            wg.at[f, at.s_side], wg.at[f, at.s_side], send_r.at[k], recv.at[f, at.s_side],
            (f, 2 * at.pair_at(k) + side),
        )

    cross = remote(
        w_ref.at[heads * (1 - side) + f], wg.at[f, s], send_x, recv.at[f, s], (f, at.s_side)
    )
    rows_out = remote(xm_ref, xg.at[side], xm_send, xm_recv, (f, at.s_side))

    def to_far(t):
        return remote(wg.at[f, t], wg.at[f, t], send_y.at[t], recv.at[f, t], (at.f_far, s))

    def to_core(t):
        return remote(wg.at[f, t], wg.at[f, t], send_c.at[t], recv.at[f, t], (at.f_core, s))

    def far_to_core(t):
        g = at.f_far
        return remote(wg.at[g, t], wg.at[g, t], send_d.at[t], recv.at[g, t], (at.f_core, s))

    def arrived(g, t):
        remote(wg.at[g, t], wg.at[g, t], send_x, recv.at[g, t], (at.f_core, s)).wait_recv()

    cross.start()
    for k in range(1, at.pairs):
        direct(k).start()
    rows_out.start()
    own = pltpu.make_async_copy(w_ref.at[pl.ds(heads * side, heads)], wg.at[:, s], local_sem.at[0])
    own.start()
    own_rows = pltpu.make_async_copy(xm_ref, xg.at[side], local_sem.at[1])
    own_rows.start()

    def forward(q):
        t = at.shard_at(q)
        arrived(f, t)

        @pl.when(q == 1)
        def _():
            for k in range(1, at.pairs):
                relay(k).start()

        to_far(t).start()
        to_core(t).start()

    def forward_far(q):
        t = at.shard_at(q)
        arrived(at.f_far, t)
        far_to_core(t).start()

    @pl.loop(1, space)
    def _(q):
        forward(q)

        @pl.when(q >= 2)
        def _():
            forward_far(q - 1)

    forward_far(space - 1)

    @pl.loop(1, space)
    def _(q):
        t = at.shard_at(q)
        arrived(at.f_core, t)
        arrived(at.f_diag, t)

    own.wait()
    own_rows.wait()
    remote(xm_ref, xg.at[1 - side], xm_send, xm_recv, (f, at.s_side)).wait_recv()

    @pl.loop(0, heads)
    def _(h):
        gain = gain_ref[heads * side + h]
        w = wg[h].reshape(-1, 3 * hd)
        for x in range(2):
            out = jnp.dot(xg[x], w, preferred_element_type=jnp.float32)
            query = out[:, :hd]
            key = out[:, hd : 2 * hd]
            query = (
                query * lax.rsqrt(jnp.mean(query * query, axis=-1, keepdims=True) + 1e-06) * gain
            )
            key = key * lax.rsqrt(jnp.mean(key * key, axis=-1, keepdims=True) + 1e-06)
            query = query.astype(jnp.bfloat16)
            key = key.astype(jnp.bfloat16)
            value = out[:, 2 * hd :].astype(jnp.bfloat16)
            for i in range(frames):
                part = slice(i * block, (i + 1) * block)
                spot = pl.ds(x * block, block)
                q_ref[i, h, spot, :] = query[part]
                kv_ref[0, i, h, spot, :] = key[part]
                kv_ref[1, i, h, spot, :] = value[part]

    cross.wait_send()
    rows_out.wait_send()
    for k in range(1, at.pairs):
        direct(k).wait_send()
        relay(k).wait_send()

    @pl.loop(1, space)
    def _(q):
        t = at.shard_at(q)
        to_far(t).wait_send()
        to_core(t).wait_send()
        far_to_core(t).wait_send()


def attend_kernel(
    space, coef_ref, q_ref, kv_ref, wo_ref, x_ref, out_ref, win, past, wog, o_own, og,
    local_sem, halo_send, halo_recv, past_send, past_recv, o_send, o_recv,
    send_a, send_x, send_y, send_c, send_d, recv,
):
    at = Place(space)
    frames, heads, tokens, hd = q_ref.shape
    block = tokens // 2
    cols = wog.shape[0]
    f, s, side = at.f, at.s, at.side
    inv = 1.0 / math.sqrt(hd)
    greet(at)

    before = (f, 2 * at.pair_at(at.pairs - 1) + side)
    after = (f, 2 * at.pair_at(1) + side)
    down = remote(
        kv_ref.at[:, :, :, pl.ds(0, block)],
        win.at[:, :, :, pl.ds(3 * block, block)],
        halo_send.at[0], halo_recv.at[0], before,
    )
    up = remote(
        kv_ref.at[:, :, :, pl.ds(block, block)],
        win.at[:, :, :, pl.ds(0, block)],
        halo_send.at[1], halo_recv.at[1], after,
    )
    far = remote(kv_ref, past.at[f], past_send.at[0], past_recv.at[f], (at.f_far, s))
    near = remote(kv_ref, past.at[f], past_send.at[1], past_recv.at[f], (at.f_core, s))
    passed = remote(
        past.at[at.f_far], past.at[at.f_far], past_send.at[2], past_recv.at[at.f_far],
        (at.f_core, s),
    )
    down.start()
    up.start()
    far.start()
    near.start()
    own_win = pltpu.make_async_copy(kv_ref, win.at[:, :, :, pl.ds(block, tokens)], local_sem.at[0])
    own_win.start()
    own_past = pltpu.make_async_copy(kv_ref, past.at[f], local_sem.at[1])
    own_past.start()
    own_wo = pltpu.make_async_copy(wo_ref, wog.at[:, s], local_sem.at[2])
    own_wo.start()

    def direct(k):
        return remote(
            wo_ref.at[f], wog.at[f, s], send_a.at[k], recv.at[f, s],
            (f, 2 * at.pair_at(k) + side),
        )

    def to_side(k):
        t = 2 * at.pair_at(k) + side
        return remote(wog.at[f, t], wog.at[f, t], send_x.at[k], recv.at[f, t], (f, at.s_side))

    def to_far(t):
        return remote(wog.at[f, t], wog.at[f, t], send_y.at[t], recv.at[f, t], (at.f_far, s))

    def to_core(t):
        return remote(wog.at[f, t], wog.at[f, t], send_c.at[t], recv.at[f, t], (at.f_core, s))

    def far_to_core(t):
        g = at.f_far
        return remote(wog.at[g, t], wog.at[g, t], send_d.at[t], recv.at[g, t], (at.f_core, s))

    def arrived(g, t):
        remote(wog.at[g, t], wog.at[g, t], o_send, recv.at[g, t], (at.f_core, s)).wait_recv()

    first = remote(wo_ref.at[f], wog.at[f, s], send_x.at[0], recv.at[f, s], (f, at.s_side))
    first.start()
    for k in range(1, at.pairs):
        direct(k).start()

    @pl.loop(1, space)
    def _(q):
        t = at.shard_at(q)
        arrived(f, t)

        @pl.when(lax.rem(q, 2) == 0)
        def _():
            to_side(q // 2).start()

        to_far(t).start()
        to_core(t).start()

    remote(kv_ref, past.at[at.f_far], o_send, past_recv.at[at.f_far], (at.f_core, s)).wait_recv()
    passed.start()

    @pl.loop(1, space)
    def _(q):
        t = at.shard_at(q)
        arrived(at.f_far, t)
        far_to_core(t).start()

    down.wait_recv()
    up.wait_recv()
    own_win.wait()
    own_past.wait()
    for g in (at.f_core, at.f_diag):
        remote(kv_ref, past.at[g], o_send, past_recv.at[g], (at.f_core, s)).wait_recv()

    lead = lax.broadcasted_iota(jnp.int32, (block, 3 * block), 1)
    back = lax.broadcasted_iota(jnp.int32, (block, 3 * block), 0)
    band = jnp.abs(lead - back - block) <= block

    @pl.loop(0, 2 * frames)
    def _(n):
        i = n // 2
        b = lax.rem(n, 2)
        mine = f * frames + i
        tok = pl.ds(pl.multiple_of(b * block, block), block)
        wide = pl.ds(pl.multiple_of(b * block, block), 3 * block)
        for h in range(heads):
            q = q_ref[i, h, tok, :]
            score = (
                lax.dot_general(
                    q, win[0, i, h, wide, :], (((1,), (1,)), ((), ())),
                    preferred_element_type=jnp.float32,
                )
                * inv
            )
            score = jnp.where(band, score, -1e30)
            top = jnp.max(score, axis=-1, keepdims=True)
            q32 = q.astype(jnp.float32)
            times = []
            for g in range(4 * frames):
                k_g = past[g // frames, 0, g % frames, h, tok, :].astype(jnp.float32)
                t_g = jnp.sum(q32 * k_g, axis=-1, keepdims=True) * inv
                t_g = jnp.where(g < mine, t_g, -1e30)
                top = jnp.maximum(top, t_g)
                times.append(t_g)
            p = jnp.where(band, jnp.exp(score - top), 0.0)
            total = jnp.sum(p, axis=-1, keepdims=True)
            acc = jnp.dot(
                p.astype(jnp.bfloat16), win[1, i, h, wide, :], preferred_element_type=jnp.float32
            )
            for g in range(4 * frames):
                p_g = jnp.where(g < mine, jnp.exp(times[g] - top), 0.0)
                total = total + p_g
                v_g = past[g // frames, 1, g % frames, h, tok, :].astype(jnp.float32)
                acc = acc + p_g.astype(jnp.bfloat16).astype(jnp.float32) * v_g
            o_own[b, i, :, h * hd : (h + 1) * hd] = (acc / total).astype(jnp.bfloat16)

    swap = remote(o_own.at[1 - side], og.at[side], o_send, o_recv, (f, at.s_side))
    swap.start()
    keep = pltpu.make_async_copy(o_own.at[side], og.at[side], local_sem.at[3])
    keep.start()

    @pl.loop(1, space)
    def _(q):
        t = at.shard_at(q)
        arrived(at.f_core, t)
        arrived(at.f_diag, t)

    own_wo.wait()
    keep.wait()
    remote(o_own.at[0], og.at[1 - side], o_send, o_recv, (f, at.s_side)).wait_recv()

    width = wog.shape[3]
    for c in range(cols):
        w = wog[c].reshape(2, heads * hd, width)
        spot = slice(c * width, (c + 1) * width)
        for i in range(frames):
            proj = jnp.dot(og[0, i], w[0], preferred_element_type=jnp.float32)
            proj = proj + jnp.dot(og[1, i], w[1], preferred_element_type=jnp.float32)
            x32 = x_ref[i, :, spot].astype(jnp.float32)
            eps = x32 + proj
            clean = (x32 - coef_ref[i, 0] * eps) / coef_ref[i, 1]
            out_ref[i, :, spot] = (coef_ref[i, 2] * clean + coef_ref[i, 3] * eps).astype(
                jnp.bfloat16
            )

    for copy in (down, up, far, near, passed, first, swap):
        copy.wait_send()
    for k in range(1, at.pairs):
        direct(k).wait_send()
        to_side(k).wait_send()

    @pl.loop(1, space)
    def _(q):
        t = at.shard_at(q)
        to_far(t).wait_send()
        to_core(t).wait_send()
        far_to_core(t).wait_send()


def body(frames_in, levels, fresh, w_mod, w_qkv, q_gain, w_out):
    space = lax.axis_size("space")
    frame_count = lax.axis_size("frame")
    local_frames, rows, width = frames_in.shape
    heads = q_gain.shape[0]
    hd = w_qkv.shape[1] // (3 * heads)
    half = heads // 2
    bf16 = jnp.bfloat16
    vmem = pl.BlockSpec(memory_space=pltpu.VMEM)
    smem = pl.BlockSpec(memory_space=pltpu.SMEM)
    dma = pltpu.SemaphoreType.DMA

    mod = jnp.dot(embed(levels, w_mod.shape[0]), w_mod, preferred_element_type=jnp.float32)
    shift = mod[:, :width]
    scale = mod[:, width:]
    x32 = frames_in.astype(jnp.float32)
    mean = jnp.mean(x32, axis=-1, keepdims=True)
    var = jnp.mean((x32 - mean) ** 2, axis=-1, keepdims=True)
    normed = (x32 - mean) * lax.rsqrt(var + 1e-06)
    xm = (normed * (1.0 + scale[:, None, :]) + shift[:, None, :]).astype(bf16)
    xm = xm.reshape(local_frames * rows, width)

    depth = w_qkv.shape[0]
    w_heads = w_qkv.reshape(depth, 3, heads, hd).transpose(2, 0, 1, 3).reshape(heads, depth, 3 * hd)
    kv_shape = (2, local_frames, half, 2 * rows, hd)
    q, kv = pl.pallas_call(
        functools.partial(qkv_kernel, space),
        out_shape=(
            jax.ShapeDtypeStruct((local_frames, half, 2 * rows, hd), bf16),
            jax.ShapeDtypeStruct(kv_shape, bf16),
        ),
        in_specs=[smem, vmem, vmem],
        out_specs=(vmem, vmem),
        scratch_shapes=[
            pltpu.VMEM((2, local_frames * rows, width), bf16),
            pltpu.VMEM((half, space, depth, 3 * hd), bf16),
            dma((2,)), dma, dma,
            dma((space // 2,)), dma((space // 2,)), dma,
            dma((space,)), dma((space,)), dma((space,)), dma((frame_count, space)),
        ],
        compiler_params=pltpu.CompilerParams(
            collective_id=0, has_side_effects=True, vmem_limit_bytes=VMEM_LIMIT
        ),
        name="qkv",
    )(q_gain, xm, w_heads)

    later = jnp.maximum(levels - LEVELS // FRAMES, 0)
    a_now = alpha_bar(levels)
    a_later = alpha_bar(later)
    coefs = jnp.stack(
        [jnp.sqrt(1.0 - a_now), jnp.sqrt(a_now), jnp.sqrt(a_later), jnp.sqrt(1.0 - a_later)],
        axis=1,
    )
    cols = frame_count
    wo_depth = w_out.shape[0]
    wo = w_out.reshape(wo_depth, cols, width // cols).transpose(1, 0, 2)
    denoised = pl.pallas_call(
        functools.partial(attend_kernel, space),
        out_shape=jax.ShapeDtypeStruct(frames_in.shape, bf16),
        in_specs=[smem, vmem, vmem, vmem, vmem],
        out_specs=vmem,
        scratch_shapes=[
            pltpu.VMEM((2, local_frames, half, 4 * rows, hd), bf16),
            pltpu.VMEM((frame_count,) + kv_shape, bf16),
            pltpu.VMEM((cols, space, wo_depth, width // cols), bf16),
            pltpu.VMEM((2, local_frames, rows, half * hd), bf16),
            pltpu.VMEM((2, local_frames, rows, half * hd), bf16),
            dma((4,)), dma((2,)), dma((2,)), dma((3,)), dma((frame_count,)), dma, dma,
            dma((space // 2,)), dma((space // 2,)),
            dma((space,)), dma((space,)), dma((space,)), dma((frame_count, space)),
        ],
        compiler_params=pltpu.CompilerParams(
            collective_id=1, has_side_effects=True, vmem_limit_bytes=VMEM_LIMIT
        ),
        name="attend",
    )(coefs, q, kv, wo, frames_in)

    arriving = from_behind(denoised[0:1], "frame", -1)
    is_last = lax.axis_index("frame") == frame_count - 1
    tail = jnp.where(is_last, fresh[None], arriving)
    return jnp.concatenate([denoised[1:], tail], axis=0)


def solution(mesh):
    return jax.shard_map(
        body,
        mesh=mesh,
        in_specs=(
            P("frame", "space", None),
            P("frame"),
            P("space", None),
            P(),
            P("space", None),
            P(),
            P("space", None),
        ),
        out_specs=P("frame", "space", None),
        check_vma=False,
    )
```

time: 361 us -> 177 us (0.49)
  waiting for transfers between devices: 267 us -> 10 us
  Pallas kernels: 0 us -> 141 us
  matrix products: 27.2 us -> 0.38 us
  local copies, waits for them, and re-layouts: 31.2 us -> 13.7 us
  between operations: 13.4 us -> 0.09 us
  other arithmetic: 15.6 us -> 6.84 us
    all_gather x4 -> x0, waiting for transfers between devices: 215 us -> none  [the longest x1 177 us: body(): lax.all_gather(w_qkv, 'space', axis=0, tiled=True)]
    pallas_call x0 -> x2, Pallas kernels: none -> 141 us  [the longest x1 80.6 us: body(): pl.pallas_call(functools.partial(attend_kernel, space), out_shape=jax.Sha...]
    ppermute x2 -> x0, waiting for transfers between devices: 42.9 us -> none  [the longest x1 42.4 us: with_halo(): lax.ppermute(head, axis, [((i + 1) % count, i) for i in range(count)])]
    dot_general x6 -> x0, matrix products: 26.9 us -> none  [the longest x1 7.25 us: body(): jnp.dot(columns, lax.all_gather(w_qkv, 'space', axis=0, tiled=True), pref...]
    dot_general x2 -> x0, local copies, waits for them, and re-layouts: 17.9 us -> none  [the longest x1 15.6 us: body(): jnp.dot(columns, lax.all_gather(w_qkv, 'space', axis=0, tiled=True), pref...]
    convert_element_type x4 -> x0, local copies, waits for them, and re-layouts: 5.51 us -> none  [the longest x2 2.39 us: body(): v_vals = qkv[:, :, 2].astype(jnp.bfloat16)]
    reduce_sum x3 -> x0, other arithmetic: 5.11 us -> none  [the longest x1 3.79 us: body(): sums = jnp.sum(probs, axis=-1)]
    reshape x0 -> x2, local copies, waits for them, and re-layouts: none -> 4.64 us  [the longest x1 2.6 us: body(): w_qkv.reshape(depth, 3, heads, hd).transpose(2, 0, 1, 3)]
  transfers between devices with their start and end apart: 7 -> 1, of which waited for: 5 -> 1; matrix products, arithmetic and copies ran while one was open for 10% -> 0% of each run, Pallas kernels for 0% -> 0%
where the time goes in v1:
time: 177 us; the launch traced here: 176 us
  Pallas kernels  141 us (80%)
  local copies, waits for them, and re-layouts  13.7 us (8%)
  waiting for transfers between devices  10 us (6%)
  other arithmetic  6.84 us (4%)
  starting transfers between devices  4.36 us (2%)
    pallas_call x1, Pallas kernels, body(): pl.pallas_call(functools.partial(attend_kernel, space), out_shape=jax.Sha...  80.6 us
    pallas_call x1, Pallas kernels, body(): pl.pallas_call(functools.partial(qkv_kernel, space), out_shape=(jax.Shape...  60.5 us
    ppermute x1, waiting for transfers between devices, from_behind(): return lax.ppermute(array, axis, pairs)  10 us
    unnamed x6, local copies, waits for them, and re-layouts  4.65 us
    ppermute x1, starting transfers between devices, from_behind(): return lax.ppermute(array, axis, pairs)  4.36 us
  transfers between devices with their start and end apart: 1, of which 1 were waited for; matrix products, arithmetic and copies ran while one was open for 0% of the time, Pallas kernels for 0%

profile of v1, /device:TPU:1, one launch (start us, length us, event | category | flops | bytes accessed | tf_op | source)
XLA Modules:
  0.0 176.5 jit_solution(11521645934367586159)
XLA Ops:
  0.0 0.9 sqrt_bitcast_fusion.3
  0.9 0.7 convert_element_type.14
  1.7 0.1 copy.23
  1.7 0.1 copy.20
  1.8 0.1 copy.21
  1.9 0.1 copy.22
  2.0 0.1 fusion.6
  2.2 0.4 fusion.8
  2.6 0.2 convert_reduce_fusion
  2.8 0.4 fusion.2
  3.2 2.6 %copy.24 = bf16[256,3072]{0,1:T(8,128)(2,1)} copy(bf16[256,3072]{1,0:T(8,128)(2,1)} %param.11) | data formatting | bytes 3145728 | tf_op args[4]
  5.8 2.7 %copy.25 = bf16[8,256,3,128]{1,3,2,0:T(8,128)(2,1)} copy(bf16[8,256,3,128]{1,3,0,2:T(8,128)(2,1)} %bitcast.19) | data formatting | bytes 3145728 | tf_op jit(solution)/shard_map/transpose | solution.py:412
  8.5 2.6 %copy.26.w_ref = bf16[8,256,384]{2,1,0:T(8,128)(2,1)} copy(bf16[8,256,384]{1,2,0:T(8,128)(2,1)} %bitcast.18) | data formatting | bytes 3145728 | tf_op jit(solution)/shard_map/reshape | solution.py:412
  11.1 2.0 %copy.27 = bf16[128,2048]{0,1:T(8,128)(2,1)} copy(bf16[128,2048]{1,0:T(8,128)(2,1)} %param.13) | data formatting | bytes 1048576 | tf_op args[6]
  13.2 2.0 %copy.28 = bf16[128,4,512]{2,0,1:T(8,128)(2,1)} copy(bf16[128,4,512]{0,2,1:T(8,128)(2,1)} %bitcast.22) | data formatting | bytes 1048576 | tf_op jit(solution)/shard_map/reshape | solution.py:444
  15.2 1.5 fusion.5
  16.7 60.5 %qkv.1 = (bf16[2,4,256,128]{3,2,1,0:T(8,128)(2,1)}, bf16[2,2,4,256,128]{4,3,2,1,0:T(8,128)(2,1)}) custom-call(f32[8]{0:T(128)} %gain_ref.1, bf16[256,2048]{1,0:T(8,128)(2,1)} %bitcast.20, bf16[8,256,384]{2,1,0:T(8,128)(2,1)} %copy.26.w_ref), custom_call_target="tpu_custom_call" | custom-call | tf_op jit(solution)/shard_map/qkv/pallas_call | solution.py:414
  77.2 0.6 pad_maximum_fusion.1.coef_ref
  77.8 80.6 %attend.1 = bf16[2,128,2048]{2,1,0:T(8,128)(2,1)} custom-call(f32[2,4]{1,0:T(2,128)} %pad_maximum_fusion.1.coef_ref, bf16[2,4,256,128]{3,2,1,0:T(8,128)(2,1)} %get-tuple-element.7.q_ref, bf16[2,2,4,256,128]{4,3,2,1,0:T(8,128)(2,1)} %get-tuple-element.8.kv_ref, bf16[4,128,512]{2,1,0:T(8,128)(2,1)} %bitcast.21, bf16[2,128,2048]{2,1,0:T(8,128)(2,1)} %x_ref.1), custom_call_target="tpu_custom_call" | custom-call | tf_op jit(solution)/shard_map/attend/pallas_call | solution.py:445
  158.4 1.3 fusion.13
  159.7 4.4 %collective-permute-start = (bf16[1,128,2048]{2,1,0:T(8,128)(2,1)S(1)}, bf16[1,128,2048]{2,1,0:T(8,128)(2,1)}, u32[]{:S(2)}, u32[]{:S(2)}) collective-permute-start(bf16[1,128,2048]{2,1,0:T(8,128)(2,1)S(1)} %get-tuple-element.12), channel_id=1, source_target_pairs={{8,0},{16,8},{24,16},{9,1},{17,9},{25,17},{10,2},{18,10},{26,18},{... | collective-permute-start | bytes 1572872 | tf_op jit(solution)/shard_map/ppermute | solution.py:20
  164.1 10.0 %collective-permute-done = bf16[1,128,2048]{2,1,0:T(8,128)(2,1)} collective-permute-done((bf16[1,128,2048]{2,1,0:T(8,128)(2,1)S(1)}, bf16[1,128,2048]{2,1,0:T(8,128)(2,1)}, u32[]{:S(2)}, u32[]{:S(2)}) %collective-permute-start) | collective-permute-done | bytes 524320 | tf_op jit(solution)/shard_map/ppermute | solution.py:20
  174.1 1.3 bitcast_select_fusion
  175.4 1.1 pad_maximum_fusion
  (9 shorter events, 0.0 us)
Async XLA Ops:
  0.0 2.1 %copy-start = (bf16[256,4096]{1,0:T(8,128)(2,1)S(1)}, bf16[256,4096]{1,0:T(8,128)(2,1)}, u32[]{:S(2)}) copy-start(bf16[256,4096]{1,0:T(8,128)(2,1)} %param.10) | copy-start | bytes 6291460
  0.0 2.6 %copy-start.1 = (bf16[2,128,2048]{2,1,0:T(8,128)(2,1)S(1)}, bf16[2,128,2048]{2,1,0:T(8,128)(2,1)}, u32[]{:S(2)}) copy-start(bf16[2,128,2048]{2,1,0:T(8,128)(2,1)} %x_ref.1) | copy-start | bytes 3145732
  159.7 14.4 %collective-permute-start = (bf16[1,128,2048]{2,1,0:T(8,128)(2,1)S(1)}, bf16[1,128,2048]{2,1,0:T(8,128)(2,1)}, u32[]{:S(2)}, u32[]{:S(2)}) collective-permute-start(bf16[1,128,2048]{2,1,0:T(8,128)(2,1)S(1)} %get-tuple-element.12), channel_id=1, source_target_pairs={{8,0},{16,8},{24,16},{9,1},{17,9},{25,17},{10,2},{18,10},{26,18},{... | collective-permute-start | bytes 1572872 | tf_op jit(solution)/shard_map/ppermute | solution.py:20

commit v2 on v0

v2 whole, which is shorter than its diff:
```python
import functools
import math

import jax
import jax.numpy as jnp
from jax import lax
from jax.experimental import pallas as pl
from jax.experimental.pallas import tpu as pltpu
from jax.sharding import PartitionSpec as P

LEVELS = 1000
FRAMES = 8
MESH = pl.DeviceIdType.MESH
VMEM_LIMIT = 56 * 1024 * 1024


def from_behind(array, axis, by):
    count = lax.axis_size(axis)
    pairs = [(i, i + by) for i in range(count) if 0 <= i + by < count]
    return lax.ppermute(array, axis, pairs)


def embed(levels, freq_count):
    half = freq_count // 2
    freqs = jnp.exp(-math.log(10000.0) * jnp.arange(half, dtype=jnp.float32) / half)
    angles = levels.astype(jnp.float32)[:, None] * freqs[None, :]
    return jnp.concatenate([jnp.cos(angles), jnp.sin(angles)], axis=1).astype(jnp.bfloat16)


def alpha_bar(steps):
    frac = steps.astype(jnp.float32) / LEVELS
    return jnp.cos((frac + 0.008) / 1.008 * (math.pi / 2)) ** 2


class Place:
    def __init__(self, space):
        self.pairs = space // 2
        self.f = lax.axis_index("frame")
        self.s = lax.axis_index("space")
        self.pair = self.s // 2
        self.side = self.s % 2
        core = self.f % 2
        self.f_core = self.f + 1 - 2 * core
        self.f_far = (self.f + 2) % 4
        self.f_diag = (self.f_core + 2) % 4
        self.s_side = self.s + 1 - 2 * self.side

    def beside(self, step):
        return 2 * lax.rem(self.pair + step + self.pairs, self.pairs) + self.side

    def onward(self, way, act):
        if way == 0:
            pl.when(self.pair + 1 < self.pairs)(lambda: act(self.s + 2))
        else:
            pl.when(self.pair >= 1)(lambda: act(self.s - 2))

    def at_distance(self, k, both_sides, act):
        sides = (self.side, 1 - self.side) if both_sides else (self.side,)

        @pl.when(self.pair >= k)
        def _():
            for side in sides:
                act(2 * (self.pair - k) + side, 0)

        @pl.when(self.pair + k < self.pairs)
        def _():
            for side in sides:
                act(2 * (self.pair + k) + side, 1)


def remote(src, dst, send_sem, recv_sem, device):
    return pltpu.make_async_remote_copy(
        src_ref=src,
        dst_ref=dst,
        send_sem=send_sem,
        recv_sem=recv_sem,
        device_id=device,
        device_id_type=MESH,
    )


def step_kernel(
    space, gain_ref, coef_ref, shift_ref, scale_ref, x_ref, w_ref, wo_ref, out_ref,
    xg, wg, wog, win, past, q_own, o_own, og,
    own_w_sem, own_wo_sem, xm_send, xm_recv,
    w_cross, w_chain, w_far, w_core, w_pass, w_recv,
    wo_chain, wo_far, wo_side, wo_core, wo_recv,
    halo_send, halo_recv, past_send, past_recv, o_keep, o_send, o_recv,
):
    at = Place(space)
    frames, rows, width = x_ref.shape
    heads, hd = og.shape[1], og.shape[4]
    inner = 2 * heads * hd
    tokens = 2 * rows
    f, s, side = at.f, at.s, at.side
    inv = 1.0 / math.sqrt(hd)

    barrier = pltpu.get_barrier_semaphore()
    partners = (
        (f, at.beside(1)), (f, at.beside(-1)), (f, at.s_side), (at.f_far, s), (at.f_core, s)
    )
    for partner in partners:
        pl.semaphore_signal(barrier, inc=1, device_id=partner, device_id_type=MESH)
    pl.semaphore_wait(barrier, len(partners))

    def columns(g, head):
        return w_ref.at[:, pl.ds(pl.multiple_of(g * inner + head * hd, hd), hd)]

    def own_w(g, h):
        return pltpu.make_async_copy(
            columns(g, heads * side + h), wg.at[g, h, s], own_w_sem.at[g, h]
        )

    def w_move(g, col, t, sem, device):
        piece = wg.at[g, col, t]
        return remote(piece, piece, sem, w_recv.at[g, col, t], device)

    def w_cross_copy(g):
        return remote(
            columns(g, heads * (1 - side) + f), wg.at[g, f, s], w_cross.at[g],
            w_recv.at[g, f, s], (f, at.s_side),
        )

    def w_first(g, way, to):
        return remote(
            columns(g, heads * side + f), wg.at[g, f, s], w_chain.at[g, s, way],
            w_recv.at[g, f, s], (f, to),
        )

    def w_next(g, t, way, to):
        return w_move(g, f, t, w_chain.at[g, t, way], (f, to))

    def w_to_far(g, t):
        return w_move(g, f, t, w_far.at[g, t], (at.f_far, s))

    def w_to_core(g, t):
        return w_move(g, f, t, w_core.at[g, t], (at.f_core, s))

    def w_passed(g, t):
        return w_move(g, at.f_far, t, w_pass.at[g, t], (at.f_core, s))

    def w_arrived(g, col, t):
        w_move(g, col, t, w_cross.at[g], (at.f_core, s)).wait_recv()

    def w_start(g):
        w_cross_copy(g).start()
        for way in (0, 1):
            at.onward(way, lambda to: w_first(g, way, to).start())
        for h in range(heads):
            own_w(g, h).start()

    def w_share(g, t):
        w_to_far(g, t).start()
        w_to_core(g, t).start()

    def w_spread(g):
        def take(t, way):
            w_arrived(g, f, t)
            at.onward(way, lambda to: w_next(g, t, way, to).start())
            w_share(g, t)

        def take_far(t, way):
            w_arrived(g, at.f_far, t)
            w_passed(g, t).start()

        w_arrived(g, f, at.s_side)
        for way in (0, 1):
            at.onward(way, lambda to: w_next(g, at.s_side, way, to).start())
        w_share(g, at.s_side)

        @pl.loop(1, at.pairs)
        def _(k):
            at.at_distance(k, True, take)

            @pl.when(k == 1)
            def _():
                take_far(at.s_side, 0)

            @pl.when(k >= 2)
            def _():
                at.at_distance(k - 1, True, take_far)

        at.at_distance(at.pairs - 1, True, take_far)

    def others(act):
        @pl.loop(0, space)
        def _(t):
            pl.when(t != s)(lambda: act(t))

    def w_complete(g):
        def both(t):
            w_arrived(g, at.f_core, t)
            w_arrived(g, at.f_diag, t)

        others(both)
        for h in range(heads):
            own_w(g, h).wait()

    def w_finish(g):
        w_cross_copy(g).wait_send()
        for way in (0, 1):
            at.onward(way, lambda to: w_first(g, way, to).wait_send())
            at.onward(way, lambda to: w_next(g, at.s_side, way, to).wait_send())

        def chain(t, way):
            at.onward(way, lambda to: w_next(g, t, way, to).wait_send())

        @pl.loop(1, at.pairs)
        def _(k):
            at.at_distance(k, True, chain)

        def shared(t):
            w_to_far(g, t).wait_send()
            w_to_core(g, t).wait_send()
            w_passed(g, t).wait_send()

        others(shared)

    cols = wog.shape[0]
    part = width // cols

    def wo_block(col):
        return wo_ref.at[:, pl.ds(pl.multiple_of(col * part, part), part)]

    def own_wo(c):
        return pltpu.make_async_copy(wo_block(c), wog.at[c, s], own_wo_sem.at[c])

    def wo_move(col, t, sem, device):
        piece = wog.at[col, t]
        return remote(piece, piece, sem, wo_recv.at[col, t], device)

    def wo_first(way, to):
        return remote(
            wo_block(f), wog.at[f, s], wo_chain.at[s, way], wo_recv.at[f, s], (f, to)
        )

    def wo_own_side(n):
        col = (f, at.f_far)[n]
        return remote(
            wo_block(col), wog.at[col, s], wo_side.at[n, s], wo_recv.at[col, s], (f, at.s_side)
        )

    def wo_next(t, way, to):
        return wo_move(f, t, wo_chain.at[t, way], (f, to))

    def wo_to_far(t):
        return wo_move(f, t, wo_far.at[t], (at.f_far, s))

    def wo_to_side(n, t):
        return wo_move((f, at.f_far)[n], t, wo_side.at[n, t], (f, at.s_side))

    def wo_to_core(n, t):
        return wo_move((f, at.f_far)[n], t, wo_core.at[n, t], (at.f_core, s))

    def wo_arrived(col, t):
        wo_move(col, t, o_keep, (at.f_core, s)).wait_recv()

    def wo_start():
        for way in (0, 1):
            at.onward(way, lambda to: wo_first(way, to).start())
        for n in (0, 1):
            wo_own_side(n).start()
        for c in range(cols):
            own_wo(c).start()

    def wo_spread():
        def take(t, way):
            wo_arrived(f, t)
            at.onward(way, lambda to: wo_next(t, way, to).start())
            wo_to_far(t).start()
            wo_to_side(0, t).start()
            wo_to_core(0, t).start()

        @pl.loop(1, at.pairs)
        def _(k):
            at.at_distance(k, False, take)

    def wo_pass_far():
        def take(t, way):
            wo_arrived(at.f_far, t)
            wo_to_side(1, t).start()
            wo_to_core(1, t).start()

        @pl.loop(1, at.pairs)
        def _(k):
            at.at_distance(k, False, take)

    def wo_pass_side():
        @pl.loop(0, at.pairs)
        def _(p):
            t = 2 * p + 1 - side
            for n in (0, 1):
                wo_arrived((f, at.f_far)[n], t)
                wo_to_core(n, t).start()

    def wo_complete():
        def both(t):
            wo_arrived(at.f_core, t)
            wo_arrived(at.f_diag, t)

        others(both)
        for c in range(cols):
            own_wo(c).wait()

    def wo_finish():
        for way in (0, 1):
            at.onward(way, lambda to: wo_first(way, to).wait_send())
        for n in (0, 1):
            wo_own_side(n).wait_send()

        def chain(t, way):
            at.onward(way, lambda to: wo_next(t, way, to).wait_send())
            wo_to_far(t).wait_send()
            for n in (0, 1):
                wo_to_side(n, t).wait_send()

        @pl.loop(1, at.pairs)
        def _(k):
            at.at_distance(k, False, chain)

        def shared(t):
            for n in (0, 1):
                wo_to_core(n, t).wait_send()

        others(shared)

    def down(h):
        return remote(
            win.at[h, :, :, pl.ds(rows, rows)], win.at[h, :, :, pl.ds(3 * rows, rows)],
            halo_send.at[0, h], halo_recv.at[0, h], (f, at.beside(-1)),
        )

    def up(h):
        return remote(
            win.at[h, :, :, pl.ds(2 * rows, rows)], win.at[h, :, :, pl.ds(0, rows)],
            halo_send.at[1, h], halo_recv.at[1, h], (f, at.beside(1)),
        )

    def past_move(g, h, n, device):
        piece = past.at[g, h]
        return remote(piece, piece, past_send.at[n, h], past_recv.at[g, h], device)

    def past_far(h):
        return past_move(f, h, 0, (at.f_far, s))

    def past_core(h):
        return past_move(f, h, 1, (at.f_core, s))

    def past_passed(h):
        return past_move(at.f_far, h, 2, (at.f_core, s))

    def o_swap(h):
        return remote(
            o_own.at[1 - side, h], og.at[side, h], o_send.at[h], o_recv.at[h], (f, at.s_side)
        )

    w_start(1)
    w_start(2)

    @pl.loop(0, frames * rows // 32)
    def _(n):
        per = rows // 32
        i = n // per
        spot = pl.ds(pl.multiple_of(lax.rem(n, per) * 32, 32), 32)
        x32 = x_ref[i, spot, :].astype(jnp.float32)
        mean = jnp.mean(x32, axis=-1, keepdims=True)
        var = jnp.mean((x32 - mean) ** 2, axis=-1, keepdims=True)
        normed = (x32 - mean) * lax.rsqrt(var + 1e-06)
        xm = normed * (1.0 + scale_ref[pl.ds(i, 1), :]) + shift_ref[pl.ds(i, 1), :]
        xg[side, pl.ds(pl.multiple_of(n * 32, 32), 32), :] = xm.astype(jnp.bfloat16)

    rows_out = remote(xg.at[side], xg.at[side], xm_send, xm_recv, (f, at.s_side))
    rows_out.start()
    w_spread(1)
    w_start(0)
    wo_start()
    w_spread(2)
    w_complete(1)
    w_complete(2)
    remote(xg.at[side], xg.at[1 - side], xm_send, xm_recv, (f, at.s_side)).wait_recv()

    @pl.loop(0, heads)
    def _(h):
        w = jnp.concatenate(
            [wg[1, h].reshape(-1, hd), wg[2, h].reshape(-1, hd)], axis=1
        )
        for x in range(2):
            both = jnp.dot(xg[x], w, preferred_element_type=jnp.float32)
            key = both[:, :hd]
            key = key * lax.rsqrt(jnp.mean(key * key, axis=-1, keepdims=True) + 1e-06)
            key = key.astype(jnp.bfloat16)
            value = both[:, hd:].astype(jnp.bfloat16)
            for i in range(frames):
                own = slice(i * rows, (i + 1) * rows)
                for n, array in ((0, key), (1, value)):
                    win[h, n, i, (1 + x) * rows : (2 + x) * rows, :] = array[own]
                    past[f, h, n, i, x * rows : (x + 1) * rows, :] = array[own]
        down(h).start()
        up(h).start()
        past_far(h).start()
        past_core(h).start()

    w_spread(0)
    wo_spread()
    w_complete(0)

    @pl.loop(0, heads // 2)
    def _(hp):
        w = jnp.concatenate(
            [wg[0, 2 * hp].reshape(-1, hd), wg[0, 2 * hp + 1].reshape(-1, hd)], axis=1
        )
        for x in range(2):
            both = jnp.dot(xg[x], w, preferred_element_type=jnp.float32)
            for n in range(2):
                h = 2 * hp + n
                query = both[:, n * hd : (n + 1) * hd]
                query = (
                    query
                    * lax.rsqrt(jnp.mean(query * query, axis=-1, keepdims=True) + 1e-06)
                    * gain_ref[heads * side + h]
                ).astype(jnp.bfloat16)
                for i in range(frames):
                    q_own[h, i, x * rows : (x + 1) * rows, :] = query[i * rows : (i + 1) * rows]

    lead = lax.broadcasted_iota(jnp.int32, (rows, 3 * rows), 1)
    back = lax.broadcasted_iota(jnp.int32, (rows, 3 * rows), 0)
    band = jnp.abs(lead - back - rows) <= rows
    ones = jnp.ones((2 * hd, hd), jnp.bfloat16)

    @pl.loop(0, heads)
    def _(h):
        remote(
            past.at[f, h], past.at[at.f_far, h], o_keep, past_recv.at[at.f_far, h], (at.f_core, s)
        ).wait_recv()
        past_passed(h).start()
        down(h).wait_recv()
        up(h).wait_recv()
        for g in (at.f_core, at.f_diag):
            remote(
                past.at[f, h], past.at[g, h], o_keep, past_recv.at[g, h], (at.f_core, s)
            ).wait_recv()

        @pl.loop(0, 2 * frames)
        def _(n):
            i = n // 2
            b = lax.rem(n, 2)
            mine = f * frames + i
            tok = pl.ds(pl.multiple_of(b * rows, rows), rows)
            wide = pl.ds(pl.multiple_of(b * rows, rows), 3 * rows)
            q = q_own[h, i, tok, :]
            score = (
                lax.dot_general(
                    q, win[h, 0, i, wide, :], (((1,), (1,)), ((), ())),
                    preferred_element_type=jnp.float32,
                )
                * inv
            )
            score = jnp.where(band, score, -1e30)
            top = jnp.broadcast_to(jnp.max(score, axis=-1, keepdims=True), (rows, hd))
            q32 = q.astype(jnp.float32)
            times = []
            for g in range(4 * frames):
                prod = q32 * past[g // frames, h, 0, g % frames, tok, :].astype(jnp.float32)
                high = prod.astype(jnp.bfloat16)
                low = (prod - high.astype(jnp.float32)).astype(jnp.bfloat16)
                t_g = (
                    jnp.dot(
                        jnp.concatenate([high, low], axis=1), ones,
                        preferred_element_type=jnp.float32,
                    )
                    * inv
                )
                t_g = jnp.where(g < mine, t_g, -1e30)
                top = jnp.maximum(top, t_g)
                times.append(t_g)
            wide_top = jnp.concatenate([top] * (3 * rows // hd), axis=1)
            p = jnp.where(band, jnp.exp(score - wide_top), 0.0)
            total = jnp.sum(p, axis=-1, keepdims=True)
            acc = jnp.dot(
                p.astype(jnp.bfloat16), win[h, 1, i, wide, :], preferred_element_type=jnp.float32
            )
            for g in range(4 * frames):
                p_g = jnp.where(g < mine, jnp.exp(times[g] - top), 0.0)
                total = total + p_g
                v_g = past[g // frames, h, 1, g % frames, tok, :].astype(jnp.float32)
                acc = acc + p_g.astype(jnp.bfloat16).astype(jnp.float32) * v_g
            o_own[b, h, i, :, :] = (acc / total).astype(jnp.bfloat16)

        o_swap(h).start()
        og[side, h] = o_own[side, h]

        @pl.when(h == 0)
        def _():
            wo_pass_far()
            wo_pass_side()

    wo_complete()
    for h in range(heads):
        remote(
            o_own.at[0, h], og.at[1 - side, h], o_keep, o_recv.at[h], (f, at.s_side)
        ).wait_recv()

    for i in range(frames):
        attended = jnp.concatenate(
            [og[x, h, i] for x in range(2) for h in range(heads)], axis=1
        )
        for c in range(cols):
            spot = slice(c * part, (c + 1) * part)
            w = wog[c].reshape(inner, part)
            x32 = x_ref[i, :, spot].astype(jnp.float32)
            eps = x32 + jnp.dot(attended, w, preferred_element_type=jnp.float32)
            clean = (x32 - coef_ref[i, 0] * eps) / coef_ref[i, 1]
            out_ref[i, :, spot] = (coef_ref[i, 2] * clean + coef_ref[i, 3] * eps).astype(
                jnp.bfloat16
            )

    rows_out.wait_send()
    for g in range(3):
        w_finish(g)
    wo_finish()

    @pl.loop(0, heads)
    def _(h):
        for copy in (down(h), up(h), past_far(h), past_core(h), past_passed(h), o_swap(h)):
            copy.wait_send()


def body(frames_in, levels, fresh, w_mod, w_qkv, q_gain, w_out):
    space = lax.axis_size("space")
    groups = lax.axis_size("frame")
    frames, rows, width = frames_in.shape
    heads = q_gain.shape[0]
    hd = w_qkv.shape[1] // (3 * heads)
    half = heads // 2
    bf16 = jnp.bfloat16
    vmem = pl.BlockSpec(memory_space=pltpu.VMEM)
    smem = pl.BlockSpec(memory_space=pltpu.SMEM)
    hbm = pl.BlockSpec(memory_space=pl.ANY)
    dma = pltpu.SemaphoreType.DMA

    mod = jnp.dot(embed(levels, w_mod.shape[0]), w_mod, preferred_element_type=jnp.float32)
    shift = mod[:, :width]
    scale = mod[:, width:]
    later = jnp.maximum(levels - LEVELS // FRAMES, 0)
    a_now = alpha_bar(levels)
    a_later = alpha_bar(later)
    coefs = jnp.stack(
        [jnp.sqrt(1.0 - a_now), jnp.sqrt(a_now), jnp.sqrt(a_later), jnp.sqrt(1.0 - a_later)],
        axis=1,
    )
    depth = w_qkv.shape[0]
    wo_depth = w_out.shape[0]
    denoised = pl.pallas_call(
        functools.partial(step_kernel, space),
        out_shape=jax.ShapeDtypeStruct(frames_in.shape, bf16),
        in_specs=[smem, smem, vmem, vmem, vmem, hbm, hbm],
        out_specs=vmem,
        scratch_shapes=[
            pltpu.VMEM((2, frames * rows, width), bf16),
            pltpu.VMEM((3, half, space, depth, hd), bf16),
            pltpu.VMEM((groups, space, wo_depth, width // groups), bf16),
            pltpu.VMEM((half, 2, frames, 4 * rows, hd), bf16),
            pltpu.VMEM((groups, half, 2, frames, 2 * rows, hd), bf16),
            pltpu.VMEM((half, frames, 2 * rows, hd), bf16),
            pltpu.VMEM((2, half, frames, rows, hd), bf16),
            pltpu.VMEM((2, half, frames, rows, hd), bf16),
            dma((3, half)), dma((groups,)), dma, dma,
            dma((3,)), dma((3, space, 2)), dma((3, space)), dma((3, space)), dma((3, space)),
            dma((3, half, space)),
            dma((space, 2)), dma((space,)), dma((2, space)), dma((2, space)),
            dma((groups, space)),
            dma((2, half)), dma((2, half)), dma((3, half)), dma((groups, half)),
            dma, dma((half,)), dma((half,)),
        ],
        compiler_params=pltpu.CompilerParams(
            collective_id=0, has_side_effects=True, vmem_limit_bytes=VMEM_LIMIT
        ),
        name="step",
    )(q_gain, coefs, shift, scale, frames_in, w_qkv, w_out)

    arriving = from_behind(denoised[0:1], "frame", -1)
    is_last = lax.axis_index("frame") == groups - 1
    tail = jnp.where(is_last, fresh[None], arriving)
    return jnp.concatenate([denoised[1:], tail], axis=0)


def solution(mesh):
    return jax.shard_map(
        body,
        mesh=mesh,
        in_specs=(
            P("frame", "space", None),
            P("frame"),
            P("space", None),
            P(),
            P("space", None),
            P(),
            P("space", None),
        ),
        out_specs=P("frame", "space", None),
        check_vma=False,
    )
```

time: 361 us -> 140 us (0.39)
  waiting for transfers between devices: 267 us -> 8.15 us
  Pallas kernels: 0 us -> 121 us
  local copies, waits for them, and re-layouts: 31.2 us -> 3.14 us
  matrix products: 27.2 us -> 0.38 us
  between operations: 13.4 us -> 0.06 us
  other arithmetic: 15.6 us -> 4.48 us
    all_gather x4 -> x0, waiting for transfers between devices: 215 us -> none  [the longest x1 177 us: body(): lax.all_gather(w_qkv, 'space', axis=0, tiled=True)]
    pallas_call x0 -> x1, Pallas kernels: none -> 121 us  [body(): pl.pallas_call(functools.partial(step_kernel, space), out_shape=jax.Shape...]
    ppermute x2 -> x0, waiting for transfers between devices: 42.9 us -> none  [the longest x1 42.4 us: with_halo(): lax.ppermute(head, axis, [((i + 1) % count, i) for i in range(count)])]
    dot_general x6 -> x0, matrix products: 26.9 us -> none  [the longest x1 7.25 us: body(): jnp.dot(columns, lax.all_gather(w_qkv, 'space', axis=0, tiled=True), pref...]
    dot_general x2 -> x0, local copies, waits for them, and re-layouts: 17.9 us -> none  [the longest x1 15.6 us: body(): jnp.dot(columns, lax.all_gather(w_qkv, 'space', axis=0, tiled=True), pref...]
    reduce_sum x5 -> x0, other arithmetic: 6.97 us -> none  [the longest x1 3.79 us: body(): sums = jnp.sum(probs, axis=-1)]
    convert_element_type x4 -> x0, local copies, waits for them, and re-layouts: 5.51 us -> none  [the longest x2 2.39 us: body(): v_vals = qkv[:, :, 2].astype(jnp.bfloat16)]
    unnamed x20 -> x4, local copies, waits for them, and re-layouts: 4.87 us -> 0.01 us
  transfers between devices with their start and end apart: 7 -> 1, of which waited for: 5 -> 1; matrix products, arithmetic and copies ran while one was open for 10% -> 0% of each run, Pallas kernels for 0% -> 0%
where the time goes in v2:
time: 140 us
  Pallas kernels  121 us (86%)
  waiting for transfers between devices  8.15 us (6%)
  other arithmetic  4.48 us (3%)
  local copies, waits for them, and re-layouts  3.14 us (2%)
  starting transfers between devices  2.64 us (2%)
    pallas_call x1, Pallas kernels, body(): pl.pallas_call(functools.partial(step_kernel, space), out_shape=jax.Shape...  121 us
    ppermute x1, waiting for transfers between devices, from_behind(): return lax.ppermute(array, axis, pairs)  8.15 us
  transfers between devices with their start and end apart: 1, of which 1 were waited for; matrix products, arithmetic and copies ran while one was open for 0% of the time, Pallas kernels for 0%

profile of v2, /device:TPU:1, one launch (start us, length us, event | category | flops | bytes accessed | tf_op | source)
XLA Modules:
  0.0 139.7 jit_solution(8195008485081873649)
XLA Ops:
  0.0 0.0 copy-start
  0.0 0.9 sqrt_bitcast_fusion.3
  0.9 0.7 convert_element_type.8
  1.6 0.1 copy.11
  1.7 0.1 copy.10
  1.8 0.1 copy.8
  1.8 0.1 copy.9
  1.9 0.1 fusion
  2.1 0.0 copy-done
  2.1 0.4 fusion.2
  2.4 0.6 fusion.8
  3.1 0.6 pad_maximum_fusion.1.coef_ref
  3.7 120.9 %step.1 = bf16[2,128,2048]{2,1,0:T(8,128)(2,1)} custom-call(f32[8]{0:T(128)} %gain_ref.1, f32[2,4]{1,0:T(2,128)} %pad_maximum_fusion.1.coef_ref, f32[2,2048]{1,0:T(2,128)} %get-tuple-element.10.shift_ref, f32[2,2048]{1,0:T(2,128)} %get-tuple-element.9.scale_ref, bf16[2,128,2048]{2,1,0:T(8,128)(2,1)} %x_ref.1, bf16[256,3072]{1,0:T(8,128)(2,1)} %w_ref.1, ...), custom_call_target="tpu_custom_call" | custom-call | tf_op jit(solution)/shard_map/step/pallas_call | solution.py:553
  124.6 0.0 copy-start.1
  124.6 2.1 %fusion.7 = (bf16[1,128,2048]{2,1,0:T(8,128)(2,1)S(1)}, bf16[1,128,2048]{2,1,0:T(8,128)(2,1)}) fusion(bf16[2,128,2048]{2,1,0:T(8,128)(2,1)} %step.1), kind=kLoop, calls=%fused_computation.19 | loop fusion | bytes 2097152 | tf_op jit(solution)/shard_map/slice | solution.py:584
  126.7 2.6 %collective-permute-start = (bf16[1,128,2048]{2,1,0:T(8,128)(2,1)}, bf16[1,128,2048]{2,1,0:T(8,128)(2,1)}, u32[]{:S(2)}, u32[]{:S(2)}) collective-permute-start(bf16[1,128,2048]{2,1,0:T(8,128)(2,1)} %get-tuple-element.8), channel_id=1, source_target_pairs={{8,0},{16,8},{24,16},{9,1},{17,9},{25,17},{10,2},{18,10},{26,18},{... | collective-permute-start | bytes 1572872 | tf_op jit(solution)/shard_map/ppermute | solution.py:20
  129.4 8.2 %collective-permute-done = bf16[1,128,2048]{2,1,0:T(8,128)(2,1)} collective-permute-done((bf16[1,128,2048]{2,1,0:T(8,128)(2,1)}, bf16[1,128,2048]{2,1,0:T(8,128)(2,1)}, u32[]{:S(2)}, u32[]{:S(2)}) %collective-permute-start) | collective-permute-done | bytes 524320 | tf_op jit(solution)/shard_map/ppermute | solution.py:20
  137.5 0.0 copy-done.1
  137.5 1.1 bitcast_select_fusion
  138.6 1.1 pad_maximum_fusion
  (2 shorter events, 0.0 us)
Async XLA Ops:
  0.0 2.1 %copy-start = (bf16[256,4096]{1,0:T(8,128)(2,1)S(1)}, bf16[256,4096]{1,0:T(8,128)(2,1)}, u32[]{:S(2)}) copy-start(bf16[256,4096]{1,0:T(8,128)(2,1)} %param.10) | copy-start | bytes 6291460
  124.6 13.0 %copy-start.1 = (bf16[128,2048]{1,0:T(8,128)(2,1)S(1)}, bf16[128,2048]{1,0:T(8,128)(2,1)}, u32[]{:S(2)}) copy-start(bf16[128,2048]{1,0:T(8,128)(2,1)} %param.9) | copy-start | bytes 1572868
  126.7 10.8 %collective-permute-start = (bf16[1,128,2048]{2,1,0:T(8,128)(2,1)}, bf16[1,128,2048]{2,1,0:T(8,128)(2,1)}, u32[]{:S(2)}, u32[]{:S(2)}) collective-permute-start(bf16[1,128,2048]{2,1,0:T(8,128)(2,1)} %get-tuple-element.8), channel_id=1, source_target_pairs={{8,0},{16,8},{24,16},{9,1},{17,9},{25,17},{10,2},{18,10},{26,18},{... | collective-permute-start | bytes 1572872 | tf_op jit(solution)/shard_map/ppermute | solution.py:20

commit v3 on v2

--- a/solution.py
+++ b/solution.py
@@ -12,12 +12,6 @@
 FRAMES = 8
 MESH = pl.DeviceIdType.MESH
 VMEM_LIMIT = 56 * 1024 * 1024
-
-
-def from_behind(array, axis, by):
-    count = lax.axis_size(axis)
-    pairs = [(i, i + by) for i in range(count) if 0 <= i + by < count]
-    return lax.ppermute(array, axis, pairs)
 
 
 def embed(levels, freq_count):
@@ -80,12 +74,13 @@
 
 
 def step_kernel(
-    space, gain_ref, coef_ref, shift_ref, scale_ref, x_ref, w_ref, wo_ref, out_ref,
-    xg, wg, wog, win, past, q_own, o_own, og,
+    space, gain_ref, coef_ref, emb_ref, x_ref, fresh_ref, w_ref, wo_ref, w_mod_ref, out_ref,
+    xg, wg, wog, win, past, q_own, o_own, og, mod, w_mod_own, leaving, arriving,
     own_w_sem, own_wo_sem, xm_send, xm_recv,
     w_cross, w_chain, w_far, w_core, w_pass, w_recv,
     wo_chain, wo_far, wo_side, wo_core, wo_recv,
     halo_send, halo_recv, past_send, past_recv, o_keep, o_send, o_recv,
+    mod_sem, leave_send, leave_recv,
 ):
     at = Place(space)
     frames, rows, width = x_ref.shape
@@ -97,7 +92,8 @@
 
     barrier = pltpu.get_barrier_semaphore()
     partners = (
-        (f, at.beside(1)), (f, at.beside(-1)), (f, at.s_side), (at.f_far, s), (at.f_core, s)
+        (f, at.beside(1)), (f, at.beside(-1)), (f, at.s_side), (at.f_far, s), (at.f_core, s),
+        (at.f_diag, s),
     )
     for partner in partners:
         pl.semaphore_signal(barrier, inc=1, device_id=partner, device_id_type=MESH)
@@ -143,7 +139,6 @@
         w_move(g, col, t, w_cross.at[g], (at.f_core, s)).wait_recv()
 
     def w_start(g):
-        w_cross_copy(g).start()
         for way in (0, 1):
             at.onward(way, lambda to: w_first(g, way, to).start())
         for h in range(heads):
@@ -336,26 +331,45 @@
             halo_send.at[1, h], halo_recv.at[1, h], (f, at.beside(1)),
         )
 
-    def past_move(g, h, n, device):
-        piece = past.at[g, h]
-        return remote(piece, piece, past_send.at[n, h], past_recv.at[g, h], device)
-
-    def past_far(h):
-        return past_move(f, h, 0, (at.f_far, s))
-
-    def past_core(h):
-        return past_move(f, h, 1, (at.f_core, s))
-
-    def past_passed(h):
-        return past_move(at.f_far, h, 2, (at.f_core, s))
+    def past_move(g, h, x, n, device):
+        piece = past.at[g, h, x]
+        return remote(piece, piece, past_send.at[n, h, x], past_recv.at[g, h, x], device)
+
+    def past_far(h, x):
+        return past_move(f, h, x, 0, (at.f_far, s))
+
+    def past_core(h, x):
+        return past_move(f, h, x, 1, (at.f_core, s))
+
+    def past_passed(h, x):
+        return past_move(at.f_far, h, x, 2, (at.f_core, s))
+
+    def past_arrived(g, h, x):
+        piece = past.at[g, h, x]
+        remote(piece, piece, o_keep, past_recv.at[g, h, x], (at.f_core, s)).wait_recv()
+
+    def leave(c):
+        return remote(
+            leaving.at[c], arriving.at[c], leave_send.at[c], leave_recv.at[c],
+            (lax.rem(f + 3, 4), s),
+        )
 
     def o_swap(h):
         return remote(
             o_own.at[1 - side, h], og.at[side, h], o_send.at[h], o_recv.at[h], (f, at.s_side)
         )
 
+    for g in (1, 2, 0):
+        w_cross_copy(g).start()
     w_start(1)
     w_start(2)
+    fetch = pltpu.make_async_copy(w_mod_ref, w_mod_own, mod_sem)
+    fetch.start()
+    fetch.wait()
+    for c in range(0, 2 * width, width // 2):
+        mod[:, c : c + width // 2] = jnp.dot(
+            emb_ref[...], w_mod_own[:, c : c + width // 2], preferred_element_type=jnp.float32
+        )
 
     @pl.loop(0, frames * rows // 32)
     def _(n):
@@ -366,41 +380,42 @@
         mean = jnp.mean(x32, axis=-1, keepdims=True)
         var = jnp.mean((x32 - mean) ** 2, axis=-1, keepdims=True)
         normed = (x32 - mean) * lax.rsqrt(var + 1e-06)
-        xm = normed * (1.0 + scale_ref[pl.ds(i, 1), :]) + shift_ref[pl.ds(i, 1), :]
+        xm = normed * (1.0 + mod[pl.ds(i, 1), width:]) + mod[pl.ds(i, 1), :width]
         xg[side, pl.ds(pl.multiple_of(n * 32, 32), 32), :] = xm.astype(jnp.bfloat16)
 
     rows_out = remote(xg.at[side], xg.at[side], xm_send, xm_recv, (f, at.s_side))
     rows_out.start()
     w_spread(1)
     w_start(0)
+    w_spread(2)
     wo_start()
-    w_spread(2)
     w_complete(1)
     w_complete(2)
-    remote(xg.at[side], xg.at[1 - side], xm_send, xm_recv, (f, at.s_side)).wait_recv()
-
-    @pl.loop(0, heads)
-    def _(h):
-        w = jnp.concatenate(
-            [wg[1, h].reshape(-1, hd), wg[2, h].reshape(-1, hd)], axis=1
-        )
-        for x in range(2):
+
+    def keys_values(x):
+        @pl.loop(0, heads)
+        def _(h):
+            w = jnp.concatenate([wg[1, h].reshape(-1, hd), wg[2, h].reshape(-1, hd)], axis=1)
             both = jnp.dot(xg[x], w, preferred_element_type=jnp.float32)
             key = both[:, :hd]
             key = key * lax.rsqrt(jnp.mean(key * key, axis=-1, keepdims=True) + 1e-06)
             key = key.astype(jnp.bfloat16)
             value = both[:, hd:].astype(jnp.bfloat16)
+            spot = pl.ds(pl.multiple_of((1 + x) * rows, rows), rows)
             for i in range(frames):
                 own = slice(i * rows, (i + 1) * rows)
                 for n, array in ((0, key), (1, value)):
-                    win[h, n, i, (1 + x) * rows : (2 + x) * rows, :] = array[own]
-                    past[f, h, n, i, x * rows : (x + 1) * rows, :] = array[own]
-        down(h).start()
-        up(h).start()
-        past_far(h).start()
-        past_core(h).start()
-
+                    win[h, n, i, spot, :] = array[own]
+                    past[f, h, x, n, i] = array[own]
+            pl.when(x == 0)(lambda: down(h).start())
+            pl.when(x == 1)(lambda: up(h).start())
+            past_far(h, x).start()
+            past_core(h, x).start()
+
+    keys_values(side)
     w_spread(0)
+    remote(xg.at[side], xg.at[1 - side], xm_send, xm_recv, (f, at.s_side)).wait_recv()
+    keys_values(1 - side)
     wo_spread()
     w_complete(0)
 
@@ -429,21 +444,19 @@
 
     @pl.loop(0, heads)
     def _(h):
-        remote(
-            past.at[f, h], past.at[at.f_far, h], o_keep, past_recv.at[at.f_far, h], (at.f_core, s)
-        ).wait_recv()
-        past_passed(h).start()
+        for x in range(2):
+            past_arrived(at.f_far, h, x)
+            past_passed(h, x).start()
         down(h).wait_recv()
         up(h).wait_recv()
         for g in (at.f_core, at.f_diag):
-            remote(
-                past.at[f, h], past.at[g, h], o_keep, past_recv.at[g, h], (at.f_core, s)
-            ).wait_recv()
+            for x in range(2):
+                past_arrived(g, h, x)
 
         @pl.loop(0, 2 * frames)
         def _(n):
-            i = n // 2
-            b = lax.rem(n, 2)
+            i = lax.rem(n, frames)
+            b = lax.rem(n // frames + 1 - side, 2)
             mine = f * frames + i
             tok = pl.ds(pl.multiple_of(b * rows, rows), rows)
             wide = pl.ds(pl.multiple_of(b * rows, rows), 3 * rows)
@@ -460,7 +473,7 @@
             q32 = q.astype(jnp.float32)
             times = []
             for g in range(4 * frames):
-                prod = q32 * past[g // frames, h, 0, g % frames, tok, :].astype(jnp.float32)
+                prod = q32 * past[g // frames, h, b, 0, g % frames].astype(jnp.float32)
                 high = prod.astype(jnp.bfloat16)
                 low = (prod - high.astype(jnp.float32)).astype(jnp.bfloat16)
                 t_g = (
@@ -482,11 +495,14 @@
             for g in range(4 * frames):
                 p_g = jnp.where(g < mine, jnp.exp(times[g] - top), 0.0)
                 total = total + p_g
-                v_g = past[g // frames, h, 1, g % frames, tok, :].astype(jnp.float32)
+                v_g = past[g // frames, h, b, 1, g % frames].astype(jnp.float32)
                 acc = acc + p_g.astype(jnp.bfloat16).astype(jnp.float32) * v_g
             o_own[b, h, i, :, :] = (acc / total).astype(jnp.bfloat16)
 
-        o_swap(h).start()
+            @pl.when(n == frames - 1)
+            def _():
+                o_swap(h).start()
+
         og[side, h] = o_own[side, h]
 
         @pl.when(h == 0)
@@ -500,20 +516,37 @@
             o_own.at[0, h], og.at[1 - side, h], o_keep, o_recv.at[h], (f, at.s_side)
         ).wait_recv()
 
-    for i in range(frames):
-        attended = jnp.concatenate(
-            [og[x, h, i] for x in range(2) for h in range(heads)], axis=1
-        )
-        for c in range(cols):
-            spot = slice(c * part, (c + 1) * part)
-            w = wog[c].reshape(inner, part)
+    attended = jnp.concatenate(
+        [og[x, h].reshape(frames * rows, hd) for x in range(2) for h in range(heads)], axis=1
+    )
+    for c in range(cols):
+        spot = slice(c * part, (c + 1) * part)
+        w = wog[c].reshape(inner, part)
+        proj = jnp.dot(attended, w, preferred_element_type=jnp.float32)
+        for i in range(frames):
             x32 = x_ref[i, :, spot].astype(jnp.float32)
-            eps = x32 + jnp.dot(attended, w, preferred_element_type=jnp.float32)
-            clean = (x32 - coef_ref[i, 0] * eps) / coef_ref[i, 1]
-            out_ref[i, :, spot] = (coef_ref[i, 2] * clean + coef_ref[i, 3] * eps).astype(
-                jnp.bfloat16
-            )
-
+            eps = x32 + proj[i * rows : (i + 1) * rows]
+            clean = (x32 - coef_ref[0, i] * eps) / coef_ref[1, i]
+            done = (coef_ref[2, i] * clean + coef_ref[3, i] * eps).astype(jnp.bfloat16)
+            if i == 0:
+                leaving[c] = done
+                leave(c).start()
+            else:
+                out_ref[i - 1, :, spot] = done
+
+    @pl.when(f == 3)
+    def _():
+        out_ref[frames - 1] = fresh_ref[...]
+
+    for c in range(cols):
+        leave(c).wait_recv()
+
+        @pl.when(f != 3)
+        def _():
+            out_ref[frames - 1, :, c * part : (c + 1) * part] = arriving[c]
+
+    for c in range(cols):
+        leave(c).wait_send()
     rows_out.wait_send()
     for g in range(3):
         w_finish(g)
@@ -521,8 +554,11 @@
 
     @pl.loop(0, heads)
     def _(h):
-        for copy in (down(h), up(h), past_far(h), past_core(h), past_passed(h), o_swap(h)):
+        for copy in (down(h), up(h), o_swap(h)):
             copy.wait_send()
+        for x in range(2):
+            for copy in (past_far(h, x), past_core(h, x), past_passed(h, x)):
+                copy.wait_send()
 
 
 def body(frames_in, levels, fresh, w_mod, w_qkv, q_gain, w_out):
@@ -538,50 +574,47 @@
     hbm = pl.BlockSpec(memory_space=pl.ANY)
     dma = pltpu.SemaphoreType.DMA
 
-    mod = jnp.dot(embed(levels, w_mod.shape[0]), w_mod, preferred_element_type=jnp.float32)
-    shift = mod[:, :width]
-    scale = mod[:, width:]
+    emb = embed(levels, w_mod.shape[0])
+    emb = jnp.pad(emb, ((0, 16 - frames), (0, 0)))
     later = jnp.maximum(levels - LEVELS // FRAMES, 0)
     a_now = alpha_bar(levels)
     a_later = alpha_bar(later)
     coefs = jnp.stack(
-        [jnp.sqrt(1.0 - a_now), jnp.sqrt(a_now), jnp.sqrt(a_later), jnp.sqrt(1.0 - a_later)],
-        axis=1,
+        [jnp.sqrt(1.0 - a_now), jnp.sqrt(a_now), jnp.sqrt(a_later), jnp.sqrt(1.0 - a_later)]
     )
     depth = w_qkv.shape[0]
     wo_depth = w_out.shape[0]
-    denoised = pl.pallas_call(
+    return pl.pallas_call(
         functools.partial(step_kernel, space),
         out_shape=jax.ShapeDtypeStruct(frames_in.shape, bf16),
-        in_specs=[smem, smem, vmem, vmem, vmem, hbm, hbm],
+        in_specs=[smem, smem, vmem, vmem, vmem, hbm, hbm, hbm],
         out_specs=vmem,
         scratch_shapes=[
             pltpu.VMEM((2, frames * rows, width), bf16),
             pltpu.VMEM((3, half, space, depth, hd), bf16),
             pltpu.VMEM((groups, space, wo_depth, width // groups), bf16),
             pltpu.VMEM((half, 2, frames, 4 * rows, hd), bf16),
-            pltpu.VMEM((groups, half, 2, frames, 2 * rows, hd), bf16),
+            pltpu.VMEM((groups, half, 2, 2, frames, rows, hd), bf16),
             pltpu.VMEM((half, frames, 2 * rows, hd), bf16),
             pltpu.VMEM((2, half, frames, rows, hd), bf16),
             pltpu.VMEM((2, half, frames, rows, hd), bf16),
+            pltpu.VMEM((16, 2 * width), jnp.float32),
+            pltpu.VMEM(w_mod.shape, bf16),
+            pltpu.VMEM((groups, rows, width // groups), bf16),
+            pltpu.VMEM((groups, rows, width // groups), bf16),
             dma((3, half)), dma((groups,)), dma, dma,
             dma((3,)), dma((3, space, 2)), dma((3, space)), dma((3, space)), dma((3, space)),
             dma((3, half, space)),
             dma((space, 2)), dma((space,)), dma((2, space)), dma((2, space)),
             dma((groups, space)),
-            dma((2, half)), dma((2, half)), dma((3, half)), dma((groups, half)),
-            dma, dma((half,)), dma((half,)),
+            dma((2, half)), dma((2, half)), dma((3, half, 2)), dma((groups, half, 2)),
+            dma, dma((half,)), dma((half,)), dma, dma((groups,)), dma((groups,)),
         ],
         compiler_params=pltpu.CompilerParams(
             collective_id=0, has_side_effects=True, vmem_limit_bytes=VMEM_LIMIT
         ),
         name="step",
-    )(q_gain, coefs, shift, scale, frames_in, w_qkv, w_out)
-
-    arriving = from_behind(denoised[0:1], "frame", -1)
-    is_last = lax.axis_index("frame") == groups - 1
-    tail = jnp.where(is_last, fresh[None], arriving)
-    return jnp.concatenate([denoised[1:], tail], axis=0)
+    )(q_gain, coefs, emb, frames_in, fresh, w_qkv, w_out, w_mod)
 
 
 def solution(mesh):

time: 140 us -> 131 us (0.936)
  waiting for transfers between devices: 8.15 us -> 0 us
  Pallas kernels: 121 us -> 125 us
  starting transfers between devices: 2.64 us -> 0 us
  other arithmetic: 4.48 us -> 2.76 us
    ppermute x1 -> x0, waiting for transfers between devices: 8.15 us -> none  [from_behind(): return lax.ppermute(array, axis, pairs)]
    pallas_call x1, Pallas kernels: 121 us -> 125 us  [body(): pl.pallas_call(functools.partial(step_kernel, space), out_shape=jax.Shape...]
    slice x2 -> x0, local copies, waits for them, and re-layouts: 2.76 us -> none  [the longest x1 2.14 us: body(): return jnp.concatenate([denoised[1:], tail], axis=0)]
    ppermute x1 -> x0, starting transfers between devices: 2.64 us -> none  [from_behind(): return lax.ppermute(array, axis, pairs)]
    unnamed x4 -> x1, local copies, waits for them, and re-layouts: 0.01 us -> 2.3 us
  transfers between devices with their start and end apart: 1 -> 0, of which waited for: 1 -> 0; matrix products, arithmetic and copies ran while one was open for 0% -> 0% of each run, Pallas kernels for 0% -> 0%
where the time goes in v3:
time: 131 us; the launch traced here: 130 us
  Pallas kernels  125 us (95%)
  other arithmetic  2.76 us (2%)
  local copies, waits for them, and re-layouts  2.3 us (2%)
    pallas_call x1, Pallas kernels, body(): pl.pallas_call(functools.partial(step_kernel, space), out_shape=jax.Shape...  125 us

profile of v3, /device:TPU:1, one launch (start us, length us, event | category | flops | bytes accessed | tf_op | source)
XLA Modules:
  0.0 130.0 jit_solution(7557390208265534164)
XLA Ops:
  0.0 0.7 convert_element_type.10
  0.7 0.1 fusion.3
  0.8 0.8 sqrt_bitcast_fusion.3
  1.6 0.6 pad_maximum_fusion.coef_ref
  2.2 0.6 fusion.2.emb_ref
  2.8 125.0 %step.1 = bf16[2,128,2048]{2,1,0:T(8,128)(2,1)} custom-call(f32[8]{0:T(128)} %gain_ref.1, f32[4,2]{1,0:T(4,128)} %pad_maximum_fusion.coef_ref, bf16[16,256]{1,0:T(8,128)(2,1)} %fusion.2.emb_ref, bf16[2,128,2048]{2,1,0:T(8,128)(2,1)} %x_ref.1, bf16[128,2048]{1,0:T(8,128)(2,1)} %fresh_ref.1, bf16[256,3072]{1,0:T(8,128)(2,1)} %w_ref.1, ...), custom_call_target="tpu_custom_call" | custom-call | tf_op jit(solution)/shard_map/step/pallas_call | solution.py:587
  127.7 2.3 %copy.9 = bf16[2,128,2048]{2,1,0:T(8,128)(2,1)} copy(bf16[2,128,2048]{2,1,0:T(8,128)(2,1)} %step.1) | data formatting | bytes 2097152
  (2 shorter events, 0.0 us)

commit v4 on v3

--- a/solution.py
+++ b/solution.py
@@ -85,6 +85,8 @@
     at = Place(space)
     frames, rows, width = x_ref.shape
     heads, hd = og.shape[1], og.shape[4]
+    groups = wog.shape[0]
+    assert rows == hd
     inner = 2 * heads * hd
     tokens = 2 * rows
     f, s, side = at.f, at.s, at.side
@@ -258,7 +260,7 @@
         for c in range(cols):
             own_wo(c).start()
 
-    def wo_spread():
+    def wo_spread(k):
         def take(t, way):
             wo_arrived(f, t)
             at.onward(way, lambda to: wo_next(t, way, to).start())
@@ -266,19 +268,15 @@
             wo_to_side(0, t).start()
             wo_to_core(0, t).start()
 
-        @pl.loop(1, at.pairs)
-        def _(k):
-            at.at_distance(k, False, take)
-
-    def wo_pass_far():
+        at.at_distance(k, False, take)
+
+    def wo_pass_far(k):
         def take(t, way):
             wo_arrived(at.f_far, t)
             wo_to_side(1, t).start()
             wo_to_core(1, t).start()
 
-        @pl.loop(1, at.pairs)
-        def _(k):
-            at.at_distance(k, False, take)
+        at.at_distance(k, False, take)
 
     def wo_pass_side():
         @pl.loop(0, at.pairs)
@@ -321,13 +319,13 @@
 
     def down(h):
         return remote(
-            win.at[h, :, :, pl.ds(rows, rows)], win.at[h, :, :, pl.ds(3 * rows, rows)],
+            win.at[h, 1], win.at[h, 3],
             halo_send.at[0, h], halo_recv.at[0, h], (f, at.beside(-1)),
         )
 
     def up(h):
         return remote(
-            win.at[h, :, :, pl.ds(2 * rows, rows)], win.at[h, :, :, pl.ds(0, rows)],
+            win.at[h, 2], win.at[h, 0],
             halo_send.at[1, h], halo_recv.at[1, h], (f, at.beside(1)),
         )
 
@@ -399,14 +397,14 @@
             both = jnp.dot(xg[x], w, preferred_element_type=jnp.float32)
             key = both[:, :hd]
             key = key * lax.rsqrt(jnp.mean(key * key, axis=-1, keepdims=True) + 1e-06)
-            key = key.astype(jnp.bfloat16)
-            value = both[:, hd:].astype(jnp.bfloat16)
-            spot = pl.ds(pl.multiple_of((1 + x) * rows, rows), rows)
             for i in range(frames):
                 own = slice(i * rows, (i + 1) * rows)
-                for n, array in ((0, key), (1, value)):
-                    win[h, n, i, spot, :] = array[own]
-                    past[f, h, x, n, i] = array[own]
+                key_t = key[own].T.astype(jnp.bfloat16)
+                value_t = both[own, hd:].T.astype(jnp.bfloat16)
+                win[h, 1 + x, 0, i] = key[own].astype(jnp.bfloat16)
+                win[h, 1 + x, 1, i] = value_t
+                past[f, h, x, 0, i] = key_t
+                past[f, h, x, 1, i] = value_t
             pl.when(x == 0)(lambda: down(h).start())
             pl.when(x == 1)(lambda: up(h).start())
             past_far(h, x).start()
@@ -416,7 +414,6 @@
     w_spread(0)
     remote(xg.at[side], xg.at[1 - side], xm_send, xm_recv, (f, at.s_side)).wait_recv()
     keys_values(1 - side)
-    wo_spread()
     w_complete(0)
 
     @pl.loop(0, heads // 2)
@@ -433,14 +430,16 @@
                     query
                     * lax.rsqrt(jnp.mean(query * query, axis=-1, keepdims=True) + 1e-06)
                     * gain_ref[heads * side + h]
-                ).astype(jnp.bfloat16)
+                )
                 for i in range(frames):
-                    q_own[h, i, x * rows : (x + 1) * rows, :] = query[i * rows : (i + 1) * rows]
-
-    lead = lax.broadcasted_iota(jnp.int32, (rows, 3 * rows), 1)
-    back = lax.broadcasted_iota(jnp.int32, (rows, 3 * rows), 0)
-    band = jnp.abs(lead - back - rows) <= rows
-    ones = jnp.ones((2 * hd, hd), jnp.bfloat16)
+                    q_own[h, x, i] = query[i * rows : (i + 1) * rows].T.astype(jnp.bfloat16)
+
+    stride = (at.pairs - 1 + heads - 1) // heads
+    kk = lax.broadcasted_iota(jnp.int32, (rows, rows), 0)
+    rr = lax.broadcasted_iota(jnp.int32, (rows, rows), 1)
+    whole = kk >= 0
+    band = jnp.concatenate([kk >= rr, whole, kk <= rr], axis=0)
+    order = lax.broadcasted_iota(jnp.int32, (groups * frames, rows), 0)
 
     @pl.loop(0, heads)
     def _(h):
@@ -458,46 +457,29 @@
             i = lax.rem(n, frames)
             b = lax.rem(n // frames + 1 - side, 2)
             mine = f * frames + i
-            tok = pl.ds(pl.multiple_of(b * rows, rows), rows)
-            wide = pl.ds(pl.multiple_of(b * rows, rows), 3 * rows)
-            q = q_own[h, i, tok, :]
-            score = (
-                lax.dot_general(
-                    q, win[h, 0, i, wide, :], (((1,), (1,)), ((), ())),
-                    preferred_element_type=jnp.float32,
-                )
-                * inv
+            q = q_own[h, b, i]
+            keys = jnp.concatenate([win[h, b + j, 0, i] for j in range(3)], axis=0)
+            score = jnp.dot(keys, q, preferred_element_type=jnp.float32) * inv
+            score = jnp.where(band, score, -1e30)
+            q32 = q.astype(jnp.float32)
+            time = jnp.full(order.shape, -1e30, jnp.float32)
+            for g in range(groups * frames):
+                k_g = past[g // frames, h, b, 0, g % frames].astype(jnp.float32)
+                t_g = jnp.sum(q32 * k_g, axis=0, keepdims=True) * inv
+                time = jnp.where(jnp.logical_and(order == g, order < mine), t_g, time)
+            top = jnp.maximum(
+                jnp.max(score, axis=0, keepdims=True), jnp.max(time, axis=0, keepdims=True)
             )
-            score = jnp.where(band, score, -1e30)
-            top = jnp.broadcast_to(jnp.max(score, axis=-1, keepdims=True), (rows, hd))
-            q32 = q.astype(jnp.float32)
-            times = []
-            for g in range(4 * frames):
-                prod = q32 * past[g // frames, h, b, 0, g % frames].astype(jnp.float32)
-                high = prod.astype(jnp.bfloat16)
-                low = (prod - high.astype(jnp.float32)).astype(jnp.bfloat16)
-                t_g = (
-                    jnp.dot(
-                        jnp.concatenate([high, low], axis=1), ones,
-                        preferred_element_type=jnp.float32,
-                    )
-                    * inv
-                )
-                t_g = jnp.where(g < mine, t_g, -1e30)
-                top = jnp.maximum(top, t_g)
-                times.append(t_g)
-            wide_top = jnp.concatenate([top] * (3 * rows // hd), axis=1)
-            p = jnp.where(band, jnp.exp(score - wide_top), 0.0)
-            total = jnp.sum(p, axis=-1, keepdims=True)
-            acc = jnp.dot(
-                p.astype(jnp.bfloat16), win[h, 1, i, wide, :], preferred_element_type=jnp.float32
-            )
-            for g in range(4 * frames):
-                p_g = jnp.where(g < mine, jnp.exp(times[g] - top), 0.0)
-                total = total + p_g
+            p = jnp.where(band, jnp.exp(score - top), 0.0)
+            p_time = jnp.where(order < mine, jnp.exp(time - top), 0.0)
+            total = jnp.sum(p, axis=0, keepdims=True) + jnp.sum(p_time, axis=0, keepdims=True)
+            values = jnp.concatenate([win[h, b + j, 1, i] for j in range(3)], axis=1)
+            acc = jnp.dot(values, p.astype(jnp.bfloat16), preferred_element_type=jnp.float32)
+            p_time = p_time.astype(jnp.bfloat16).astype(jnp.float32)
+            for g in range(groups * frames):
                 v_g = past[g // frames, h, b, 1, g % frames].astype(jnp.float32)
-                acc = acc + p_g.astype(jnp.bfloat16).astype(jnp.float32) * v_g
-            o_own[b, h, i, :, :] = (acc / total).astype(jnp.bfloat16)
+                acc = acc + p_time[g : g + 1] * v_g
+            o_own[b, h, i, :, :] = (acc / total).T.astype(jnp.bfloat16)
 
             @pl.when(n == frames - 1)
             def _():
@@ -505,11 +487,13 @@
 
         og[side, h] = o_own[side, h]
 
-        @pl.when(h == 0)
-        def _():
-            wo_pass_far()
-            wo_pass_side()
-
+        @pl.loop(h * stride + 1, jnp.minimum((h + 1) * stride, at.pairs - 1) + 1)
+        def _(k):
+            wo_spread(k)
+            pl.when(k >= 2)(lambda: wo_pass_far(k - 1))
+
+    wo_pass_far(at.pairs - 1)
+    wo_pass_side()
     wo_complete()
     for h in range(heads):
         remote(
@@ -593,9 +577,9 @@
             pltpu.VMEM((2, frames * rows, width), bf16),
             pltpu.VMEM((3, half, space, depth, hd), bf16),
             pltpu.VMEM((groups, space, wo_depth, width // groups), bf16),
-            pltpu.VMEM((half, 2, frames, 4 * rows, hd), bf16),
+            pltpu.VMEM((half, 4, 2, frames, rows, hd), bf16),
             pltpu.VMEM((groups, half, 2, 2, frames, rows, hd), bf16),
-            pltpu.VMEM((half, frames, 2 * rows, hd), bf16),
+            pltpu.VMEM((half, 2, frames, hd, rows), bf16),
             pltpu.VMEM((2, half, frames, rows, hd), bf16),
             pltpu.VMEM((2, half, frames, rows, hd), bf16),
             pltpu.VMEM((16, 2 * width), jnp.float32),

time: 131 us -> 119 us (0.908)
  Pallas kernels: 125 us -> 114 us
    pallas_call x1, Pallas kernels: 125 us -> 114 us  [body(): pl.pallas_call(functools.partial(step_kernel, space), out_shape=jax.Shape...]
where the time goes in v4:
time: 119 us
  Pallas kernels  114 us (96%)
  other arithmetic  2.76 us (2%)
  local copies, waits for them, and re-layouts  2.3 us (2%)
    pallas_call x1, Pallas kernels, body(): pl.pallas_call(functools.partial(step_kernel, space), out_shape=jax.Shape...  114 us

profile of v4, /device:TPU:1, one launch (start us, length us, event | category | flops | bytes accessed | tf_op | source)
XLA Modules:
  0.0 118.9 jit_solution(9328461941497122868)
XLA Ops:
  0.0 0.7 convert_element_type.10
  0.7 0.1 fusion.3
  0.8 0.8 sqrt_bitcast_fusion.3
  1.6 0.6 pad_maximum_fusion.coef_ref
  2.2 0.6 fusion.2.emb_ref
  2.8 113.8 %step.1 = bf16[2,128,2048]{2,1,0:T(8,128)(2,1)} custom-call(f32[8]{0:T(128)} %gain_ref.1, f32[4,2]{1,0:T(4,128)} %pad_maximum_fusion.coef_ref, bf16[16,256]{1,0:T(8,128)(2,1)} %fusion.2.emb_ref, bf16[2,128,2048]{2,1,0:T(8,128)(2,1)} %x_ref.1, bf16[128,2048]{1,0:T(8,128)(2,1)} %fresh_ref.1, bf16[256,3072]{1,0:T(8,128)(2,1)} %w_ref.1, ...), custom_call_target="tpu_custom_call" | custom-call | tf_op jit(solution)/shard_map/step/pallas_call | solution.py:571
  116.6 2.3 %copy.9 = bf16[2,128,2048]{2,1,0:T(8,128)(2,1)} copy(bf16[2,128,2048]{2,1,0:T(8,128)(2,1)} %step.1) | data formatting | bytes 2097152
  (2 shorter events, 0.0 us)

commit v5 on v4

v5 whole, which is shorter than its diff:
```python
import functools
import math

import jax
import jax.numpy as jnp
from jax import lax
from jax.experimental import pallas as pl
from jax.experimental.pallas import tpu as pltpu
from jax.sharding import PartitionSpec as P

LEVELS = 1000
FRAMES = 8
MESH = pl.DeviceIdType.MESH
VMEM_LIMIT = 56 * 1024 * 1024


def embed(levels, freq_count):
    half = freq_count // 2
    freqs = jnp.exp(-math.log(10000.0) * jnp.arange(half, dtype=jnp.float32) / half)
    angles = levels.astype(jnp.float32)[:, None] * freqs[None, :]
    return jnp.concatenate([jnp.cos(angles), jnp.sin(angles)], axis=1).astype(jnp.bfloat16)


def alpha_bar(steps):
    frac = steps.astype(jnp.float32) / LEVELS
    return jnp.cos((frac + 0.008) / 1.008 * (math.pi / 2)) ** 2


class Place:
    def __init__(self, space):
        self.pairs = space // 2
        self.f = lax.axis_index("frame")
        self.s = lax.axis_index("space")
        self.pair = self.s // 2
        self.side = self.s % 2
        core = self.f % 2
        self.f_core = self.f + 1 - 2 * core
        self.f_far = (self.f + 2) % 4
        self.f_diag = (self.f_core + 2) % 4
        self.s_side = self.s + 1 - 2 * self.side

    def beside(self, step):
        return 2 * lax.rem(self.pair + step + self.pairs, self.pairs) + self.side

    def onward(self, way, act):
        if way == 0:
            pl.when(self.pair + 1 < self.pairs)(lambda: act(self.s + 2))
        else:
            pl.when(self.pair >= 1)(lambda: act(self.s - 2))

    def at_distance(self, k, both_sides, act):
        sides = (self.side, 1 - self.side) if both_sides else (self.side,)

        @pl.when(self.pair >= k)
        def _():
            for side in sides:
                act(2 * (self.pair - k) + side, 0)

        @pl.when(self.pair + k < self.pairs)
        def _():
            for side in sides:
                act(2 * (self.pair + k) + side, 1)


def remote(src, dst, send_sem, recv_sem, device):
    return pltpu.make_async_remote_copy(
        src_ref=src,
        dst_ref=dst,
        send_sem=send_sem,
        recv_sem=recv_sem,
        device_id=device,
        device_id_type=MESH,
    )


def step_kernel(
    space, gain_ref, coef_ref, emb_ref, x_ref, fresh_ref, w_ref, wo_ref, w_mod_ref, out_ref,
    xg, wg, wx, wog, win, past, q_own, o_own, og, mod, w_mod_own, leaving, arriving,
    own_w_sem, stage_sem, own_wo_sem, xm_send, xm_recv,
    w_cross, w_chain, w_far, w_core, w_pass, w_recv,
    wo_chain, wo_far, wo_side, wo_core, wo_recv,
    halo_send, halo_recv, past_send, past_recv, o_keep, o_send, o_recv,
    mod_sem, leave_send, leave_recv,
):
    at = Place(space)
    frames, rows, width = x_ref.shape
    heads, hd = og.shape[1], og.shape[4]
    groups = wog.shape[0]
    assert rows == hd
    inner = 2 * heads * hd
    tokens = 2 * rows
    f, s, side = at.f, at.s, at.side
    inv = 1.0 / math.sqrt(hd)

    def columns(j, head):
        return w_ref.at[:, pl.ds(pl.multiple_of((j + 1) % 3 * inner + head * hd, hd), hd)]

    def own_w(j, h):
        return pltpu.make_async_copy(
            columns(j, heads * side + h), wg.at[h, s, j], own_w_sem.at[j, h]
        )

    def stage(j):
        return pltpu.make_async_copy(
            columns(j, heads * (1 - side) + f), wx.at[j], stage_sem.at[j]
        )

    slots = (pl.ds(0, 2), pl.ds(2, 1))

    def w_move(g, col, t, sem, device):
        piece = wg.at[col, t, slots[g]]
        return remote(piece, piece, sem, w_recv.at[g, col, t], device)

    def w_cross_copy(g):
        return remote(
            wx.at[slots[g]], wg.at[f, s, slots[g]], w_cross.at[g], w_recv.at[g, f, s],
            (f, at.s_side),
        )

    def w_next(g, t, way, to):
        return w_move(g, f, t, w_chain.at[g, t, way], (f, to))

    def w_to_far(g, t):
        return w_move(g, f, t, w_far.at[g, t], (at.f_far, s))

    def w_to_core(g, t):
        return w_move(g, f, t, w_core.at[g, t], (at.f_core, s))

    def w_passed(g, t):
        return w_move(g, at.f_far, t, w_pass.at[g, t], (at.f_core, s))

    def w_arrived(g, col, t):
        w_move(g, col, t, w_cross.at[g], (at.f_core, s)).wait_recv()

    def w_onward(g, t):
        for way in (0, 1):
            at.onward(way, lambda to: w_next(g, t, way, to).start())

    def w_share(g, t):
        w_to_far(g, t).start()
        w_to_core(g, t).start()

    def w_begin(g):
        w_arrived(g, f, at.s_side)
        w_onward(g, at.s_side)
        w_share(g, at.s_side)

    def w_take_far(g, t):
        w_arrived(g, at.f_far, t)
        w_passed(g, t).start()

    def w_step(g, k):
        def take(t, way):
            w_arrived(g, f, t)
            at.onward(way, lambda to: w_next(g, t, way, to).start())
            w_share(g, t)

        at.at_distance(k, True, take)
        pl.when(k == 1)(lambda: w_take_far(g, at.s_side))
        pl.when(k >= 2)(
            lambda: at.at_distance(k - 1, True, lambda t, way: w_take_far(g, t))
        )

    def w_end(g):
        at.at_distance(at.pairs - 1, True, lambda t, way: w_take_far(g, t))

    def others(act):
        @pl.loop(0, space)
        def _(t):
            pl.when(t != s)(lambda: act(t))

    def w_complete(g):
        def both(t):
            w_arrived(g, at.f_core, t)
            w_arrived(g, at.f_diag, t)

        others(both)

    def w_finish(g):
        w_cross_copy(g).wait_send()
        for t in (s, at.s_side):
            for way in (0, 1):
                at.onward(way, lambda to: w_next(g, t, way, to).wait_send())

        def chain(t, way):
            at.onward(way, lambda to: w_next(g, t, way, to).wait_send())

        @pl.loop(1, at.pairs)
        def _(k):
            at.at_distance(k, True, chain)

        def shared(t):
            w_to_far(g, t).wait_send()
            w_to_core(g, t).wait_send()
            w_passed(g, t).wait_send()

        others(shared)

    cols = wog.shape[0]
    part = width // cols

    def wo_block(col):
        return wo_ref.at[:, pl.ds(pl.multiple_of(col * part, part), part)]

    def own_wo(c):
        return pltpu.make_async_copy(wo_block(c), wog.at[c, s], own_wo_sem.at[c])

    def wo_move(col, t, sem, device):
        piece = wog.at[col, t]
        return remote(piece, piece, sem, wo_recv.at[col, t], device)

    def wo_first(way, to):
        return remote(
            wo_block(f), wog.at[f, s], wo_chain.at[s, way], wo_recv.at[f, s], (f, to)
        )

    def wo_own_side(n):
        col = (f, at.f_far)[n]
        return remote(
            wo_block(col), wog.at[col, s], wo_side.at[n, s], wo_recv.at[col, s], (f, at.s_side)
        )

    def wo_next(t, way, to):
        return wo_move(f, t, wo_chain.at[t, way], (f, to))

    def wo_to_far(t):
        return wo_move(f, t, wo_far.at[t], (at.f_far, s))

    def wo_to_side(n, t):
        return wo_move((f, at.f_far)[n], t, wo_side.at[n, t], (f, at.s_side))

    def wo_to_core(n, t):
        return wo_move((f, at.f_far)[n], t, wo_core.at[n, t], (at.f_core, s))

    def wo_arrived(col, t):
        wo_move(col, t, o_keep, (at.f_core, s)).wait_recv()

    def wo_start():
        for way in (0, 1):
            at.onward(way, lambda to: wo_first(way, to).start())
        for n in (0, 1):
            wo_own_side(n).start()
        for c in range(cols):
            own_wo(c).start()

    def wo_spread(k):
        def take(t, way):
            wo_arrived(f, t)
            at.onward(way, lambda to: wo_next(t, way, to).start())
            wo_to_far(t).start()
            wo_to_side(0, t).start()
            wo_to_core(0, t).start()

        at.at_distance(k, False, take)

    def wo_pass_far(k):
        def take(t, way):
            wo_arrived(at.f_far, t)
            wo_to_side(1, t).start()
            wo_to_core(1, t).start()

        at.at_distance(k, False, take)

    def wo_pass_side():
        @pl.loop(0, at.pairs)
        def _(p):
            t = 2 * p + 1 - side
            for n in (0, 1):
                wo_arrived((f, at.f_far)[n], t)
                wo_to_core(n, t).start()

    def wo_complete():
        def both(t):
            wo_arrived(at.f_core, t)
            wo_arrived(at.f_diag, t)

        others(both)
        for c in range(cols):
            own_wo(c).wait()

    def wo_finish():
        for way in (0, 1):
            at.onward(way, lambda to: wo_first(way, to).wait_send())
        for n in (0, 1):
            wo_own_side(n).wait_send()

        def chain(t, way):
            at.onward(way, lambda to: wo_next(t, way, to).wait_send())
            wo_to_far(t).wait_send()
            for n in (0, 1):
                wo_to_side(n, t).wait_send()

        @pl.loop(1, at.pairs)
        def _(k):
            at.at_distance(k, False, chain)

        def shared(t):
            for n in (0, 1):
                wo_to_core(n, t).wait_send()

        others(shared)

    def down(h):
        return remote(
            win.at[h, 1], win.at[h, 3],
            halo_send.at[0, h], halo_recv.at[0, h], (f, at.beside(-1)),
        )

    def up(h):
        return remote(
            win.at[h, 2], win.at[h, 0],
            halo_send.at[1, h], halo_recv.at[1, h], (f, at.beside(1)),
        )

    def past_move(g, h, x, n, device):
        piece = past.at[g, h, x]
        return remote(piece, piece, past_send.at[n, h, x], past_recv.at[g, h, x], device)

    def past_far(h, x):
        return past_move(f, h, x, 0, (at.f_far, s))

    def past_core(h, x):
        return past_move(f, h, x, 1, (at.f_core, s))

    def past_passed(h, x):
        return past_move(at.f_far, h, x, 2, (at.f_core, s))

    def past_arrived(g, h, x):
        piece = past.at[g, h, x]
        remote(piece, piece, o_keep, past_recv.at[g, h, x], (at.f_core, s)).wait_recv()

    def leave(c):
        return remote(
            leaving.at[c], arriving.at[c], leave_send.at[c], leave_recv.at[c],
            (lax.rem(f + 3, 4), s),
        )

    def o_swap(h):
        return remote(
            o_own.at[1 - side, h], og.at[side, h], o_send.at[h], o_recv.at[h], (f, at.s_side)
        )

    for j in range(3):
        stage(j).start()
    for h in range(heads):
        for j in range(3):
            own_w(j, h).start()
    fetch = pltpu.make_async_copy(w_mod_ref, w_mod_own, mod_sem)
    fetch.start()

    barrier = pltpu.get_barrier_semaphore()
    partners = (
        (f, at.beside(1)), (f, at.beside(-1)), (f, at.s_side), (at.f_far, s), (at.f_core, s),
        (at.f_diag, s),
    )
    for partner in partners:
        pl.semaphore_signal(barrier, inc=1, device_id=partner, device_id_type=MESH)
    for j in range(3):
        stage(j).wait()
    for h in range(heads):
        for j in range(3):
            own_w(j, h).wait()
    fetch.wait()
    pl.semaphore_wait(barrier, len(partners))

    for g in range(2):
        w_cross_copy(g).start()
    w_onward(0, s)
    for c in range(0, 2 * width, width // 2):
        mod[:, c : c + width // 2] = jnp.dot(
            emb_ref[...], w_mod_own[:, c : c + width // 2], preferred_element_type=jnp.float32
        )

    def send_rows(i):
        own = xg.at[side, pl.ds(i * rows, rows)]
        return remote(own, own, xm_send.at[i], xm_recv.at[i], (f, at.s_side))

    @pl.loop(0, frames * rows // 32)
    def _(n):
        per = rows // 32
        i = n // per
        spot = pl.ds(pl.multiple_of(lax.rem(n, per) * 32, 32), 32)
        x32 = x_ref[i, spot, :].astype(jnp.float32)
        mean = jnp.mean(x32, axis=-1, keepdims=True)
        var = jnp.mean((x32 - mean) ** 2, axis=-1, keepdims=True)
        normed = (x32 - mean) * lax.rsqrt(var + 1e-06)
        xm = normed * (1.0 + mod[pl.ds(i, 1), width:]) + mod[pl.ds(i, 1), :width]
        xg[side, pl.ds(pl.multiple_of(n * 32, 32), 32), :] = xm.astype(jnp.bfloat16)

        for i in range(frames):
            pl.when(n == (i + 1) * per - 1)(lambda: send_rows(i).start())

    w_begin(0)

    @pl.loop(1, at.pairs)
    def _(k):
        w_step(0, k)
        pl.when(k == 1)(lambda: w_onward(1, s))

    wo_start()
    w_end(0)
    w_complete(0)

    def keys_values(x, between):
        @pl.loop(0, heads)
        def _(h):
            w = jnp.concatenate([wg[h, :, j].reshape(-1, hd) for j in range(2)], axis=1)
            both = jnp.dot(xg[x], w, preferred_element_type=jnp.float32)
            key = both[:, :hd]
            key = key * lax.rsqrt(jnp.mean(key * key, axis=-1, keepdims=True) + 1e-06)
            for i in range(frames):
                own = slice(i * rows, (i + 1) * rows)
                key_t = key[own].T.astype(jnp.bfloat16)
                value_t = both[own, hd:].T.astype(jnp.bfloat16)
                win[h, 1 + x, 0, i] = key[own].astype(jnp.bfloat16)
                win[h, 1 + x, 1, i] = value_t
                past[f, h, x, 0, i] = key_t
                past[f, h, x, 1, i] = value_t
            pl.when(x == 0)(lambda: down(h).start())
            pl.when(x == 1)(lambda: up(h).start())
            past_far(h, x).start()
            past_core(h, x).start()
            between(h)

    stride = (at.pairs - 1 + heads - 1) // heads

    def q_steps(h):
        @pl.loop(h * stride + 1, jnp.minimum((h + 1) * stride, at.pairs - 1) + 1)
        def _(k):
            w_step(1, k)

    wo_stride = (at.pairs - 1 + 2) // 3

    def wo_steps(n):
        for k in range(n * wo_stride + 1, min((n + 1) * wo_stride, at.pairs - 1) + 1):
            wo_spread(k)
            if k >= 2:
                wo_pass_far(k - 1)

    def past_pass(h, x):
        past_arrived(at.f_far, h, x)
        past_passed(h, x).start()

    w_begin(1)
    keys_values(side, q_steps)
    w_end(1)
    wo_steps(0)
    for i in range(frames):
        other = xg.at[1 - side, pl.ds(i * rows, rows)]
        remote(other, other, xm_send.at[i], xm_recv.at[i], (f, at.s_side)).wait_recv()
    keys_values(1 - side, lambda h: None)
    wo_steps(1)
    w_complete(1)
    for h in range(heads):
        past_pass(h, side)

    @pl.loop(0, heads // 2)
    def _(hp):
        w = jnp.concatenate(
            [wg[2 * hp + n, :, 2].reshape(-1, hd) for n in range(2)], axis=1
        )
        for x in range(2):
            both = jnp.dot(xg[x], w, preferred_element_type=jnp.float32)
            for n in range(2):
                h = 2 * hp + n
                query = both[:, n * hd : (n + 1) * hd]
                query = (
                    query
                    * lax.rsqrt(jnp.mean(query * query, axis=-1, keepdims=True) + 1e-06)
                    * gain_ref[heads * side + h]
                )
                for i in range(frames):
                    q_own[h, x, i] = query[i * rows : (i + 1) * rows].T.astype(jnp.bfloat16)

    wo_steps(2)
    for i in range(frames):
        send_rows(i).wait_send()
    for g in range(2):
        w_finish(g)

    kk = lax.broadcasted_iota(jnp.int32, (rows, rows), 0)
    rr = lax.broadcasted_iota(jnp.int32, (rows, rows), 1)
    whole = kk >= 0
    band = jnp.concatenate([kk >= rr, whole, kk <= rr], axis=0)
    order = lax.broadcasted_iota(jnp.int32, (groups * frames, rows), 0)

    @pl.loop(0, heads)
    def _(h):
        past_pass(h, 1 - side)
        down(h).wait_recv()
        up(h).wait_recv()
        for g in (at.f_core, at.f_diag):
            for x in range(2):
                past_arrived(g, h, x)

        @pl.loop(0, 2 * frames)
        def _(n):
            i = lax.rem(n, frames)
            b = lax.rem(n // frames + 1 - side, 2)
            mine = f * frames + i
            q = q_own[h, b, i]
            keys = jnp.concatenate([win[h, b + j, 0, i] for j in range(3)], axis=0)
            score = jnp.dot(keys, q, preferred_element_type=jnp.float32) * inv
            score = jnp.where(band, score, -1e30)
            q32 = q.astype(jnp.float32)
            time = jnp.full(order.shape, -1e30, jnp.float32)
            for g in range(groups * frames):
                k_g = past[g // frames, h, b, 0, g % frames].astype(jnp.float32)
                t_g = jnp.sum(q32 * k_g, axis=0, keepdims=True) * inv
                time = jnp.where(jnp.logical_and(order == g, order < mine), t_g, time)
            top = jnp.maximum(
                jnp.max(score, axis=0, keepdims=True), jnp.max(time, axis=0, keepdims=True)
            )
            p = jnp.where(band, jnp.exp(score - top), 0.0)
            p_time = jnp.where(order < mine, jnp.exp(time - top), 0.0)
            total = jnp.sum(p, axis=0, keepdims=True) + jnp.sum(p_time, axis=0, keepdims=True)
            values = jnp.concatenate([win[h, b + j, 1, i] for j in range(3)], axis=1)
            acc = jnp.dot(values, p.astype(jnp.bfloat16), preferred_element_type=jnp.float32)
            p_time = p_time.astype(jnp.bfloat16).astype(jnp.float32)
            for g in range(groups * frames):
                v_g = past[g // frames, h, b, 1, g % frames].astype(jnp.float32)
                acc = acc + p_time[g : g + 1] * v_g
            o_own[b, h, i, :, :] = (acc / total).T.astype(jnp.bfloat16)

            @pl.when(n == frames - 1)
            def _():
                o_swap(h).start()

        og[side, h] = o_own[side, h]

        @pl.when(h == 0)
        def _():
            wo_pass_far(at.pairs - 1)
            wo_pass_side()

    @pl.loop(0, heads)
    def _(h):
        for copy in (down(h), up(h)):
            copy.wait_send()
        for x in range(2):
            for copy in (past_far(h, x), past_core(h, x), past_passed(h, x)):
                copy.wait_send()

    wo_complete()
    for h in range(heads):
        remote(
            o_own.at[0, h], og.at[1 - side, h], o_keep, o_recv.at[h], (f, at.s_side)
        ).wait_recv()

    attended = jnp.concatenate(
        [og[x, h].reshape(frames * rows, hd) for x in range(2) for h in range(heads)], axis=1
    )
    for c in range(cols):
        spot = slice(c * part, (c + 1) * part)
        w = wog[c].reshape(inner, part)
        proj = jnp.dot(attended, w, preferred_element_type=jnp.float32)
        for i in range(frames):
            x32 = x_ref[i, :, spot].astype(jnp.float32)
            eps = x32 + proj[i * rows : (i + 1) * rows]
            clean = (x32 - coef_ref[0, i] * eps) / coef_ref[1, i]
            done = (coef_ref[2, i] * clean + coef_ref[3, i] * eps).astype(jnp.bfloat16)
            if i == 0:
                leaving[c] = done
                leave(c).start()
            else:
                out_ref[i - 1, :, spot] = done

    @pl.when(f == 3)
    def _():
        out_ref[frames - 1] = fresh_ref[...]

    wo_finish()
    for h in range(heads):
        o_swap(h).wait_send()
    for c in range(cols):
        leave(c).wait_recv()

        @pl.when(f != 3)
        def _():
            out_ref[frames - 1, :, c * part : (c + 1) * part] = arriving[c]

    for c in range(cols):
        leave(c).wait_send()


def body(frames_in, levels, fresh, w_mod, w_qkv, q_gain, w_out):
    space = lax.axis_size("space")
    groups = lax.axis_size("frame")
    frames, rows, width = frames_in.shape
    heads = q_gain.shape[0]
    hd = w_qkv.shape[1] // (3 * heads)
    half = heads // 2
    bf16 = jnp.bfloat16
    vmem = pl.BlockSpec(memory_space=pltpu.VMEM)
    smem = pl.BlockSpec(memory_space=pltpu.SMEM)
    hbm = pl.BlockSpec(memory_space=pl.ANY)
    dma = pltpu.SemaphoreType.DMA

    emb = embed(levels, w_mod.shape[0])
    emb = jnp.pad(emb, ((0, 16 - frames), (0, 0)))
    later = jnp.maximum(levels - LEVELS // FRAMES, 0)
    a_now = alpha_bar(levels)
    a_later = alpha_bar(later)
    coefs = jnp.stack(
        [jnp.sqrt(1.0 - a_now), jnp.sqrt(a_now), jnp.sqrt(a_later), jnp.sqrt(1.0 - a_later)]
    )
    depth = w_qkv.shape[0]
    wo_depth = w_out.shape[0]
    return pl.pallas_call(
        functools.partial(step_kernel, space),
        out_shape=jax.ShapeDtypeStruct(frames_in.shape, bf16),
        in_specs=[smem, smem, vmem, vmem, vmem, hbm, hbm, hbm],
        out_specs=vmem,
        scratch_shapes=[
            pltpu.VMEM((2, frames * rows, width), bf16),
            pltpu.VMEM((half, space, 3, depth, hd), bf16),
            pltpu.VMEM((3, depth, hd), bf16),
            pltpu.VMEM((groups, space, wo_depth, width // groups), bf16),
            pltpu.VMEM((half, 4, 2, frames, rows, hd), bf16),
            pltpu.VMEM((groups, half, 2, 2, frames, rows, hd), bf16),
            pltpu.VMEM((half, 2, frames, hd, rows), bf16),
            pltpu.VMEM((2, half, frames, rows, hd), bf16),
            pltpu.VMEM((2, half, frames, rows, hd), bf16),
            pltpu.VMEM((16, 2 * width), jnp.float32),
            pltpu.VMEM(w_mod.shape, bf16),
            pltpu.VMEM((groups, rows, width // groups), bf16),
            pltpu.VMEM((groups, rows, width // groups), bf16),
            dma((3, half)), dma((3,)), dma((groups,)), dma((frames,)), dma((frames,)),
            dma((2,)), dma((2, space, 2)), dma((2, space)), dma((2, space)), dma((2, space)),
            dma((2, half, space)),
            dma((space, 2)), dma((space,)), dma((2, space)), dma((2, space)),
            dma((groups, space)),
            dma((2, half)), dma((2, half)), dma((3, half, 2)), dma((groups, half, 2)),
            dma, dma((half,)), dma((half,)), dma, dma((groups,)), dma((groups,)),
        ],
        compiler_params=pltpu.CompilerParams(
            collective_id=0, has_side_effects=True, vmem_limit_bytes=VMEM_LIMIT
        ),
        name="step",
    )(q_gain, coefs, emb, frames_in, fresh, w_qkv, w_out, w_mod)


def solution(mesh):
    return jax.shard_map(
        body,
        mesh=mesh,
        in_specs=(
            P("frame", "space", None),
            P("frame"),
            P("space", None),
            P(),
            P("space", None),
            P(),
            P("space", None),
        ),
        out_specs=P("frame", "space", None),
        check_vma=False,
    )
```

time: 119 us -> 115 us (0.966)
  Pallas kernels: 114 us -> 109 us
    pallas_call x1, Pallas kernels: 114 us -> 109 us  [body(): pl.pallas_call(functools.partial(step_kernel, space), out_shape=jax.Shape...]
where the time goes in v5:
time: 115 us; the launch traced here: 114 us
  Pallas kernels  109 us (95%)
  other arithmetic  2.76 us (2%)
  local copies, waits for them, and re-layouts  2.3 us (2%)
    pallas_call x1, Pallas kernels, body(): pl.pallas_call(functools.partial(step_kernel, space), out_shape=jax.Shape...  109 us
    unnamed x1, local copies, waits for them, and re-layouts  2.3 us

profile of v5, /device:TPU:1, one launch (start us, length us, event | category | flops | bytes accessed | tf_op | source)
XLA Modules:
  0.0 114.3 jit_solution(2797791294087156132)
XLA Ops:
  0.0 0.7 convert_element_type.10
  0.7 0.1 fusion.3
  0.8 0.8 sqrt_bitcast_fusion.3
  1.6 0.6 pad_maximum_fusion.coef_ref
  2.2 0.6 fusion.2.emb_ref
  2.8 109.2 %step.1 = bf16[2,128,2048]{2,1,0:T(8,128)(2,1)} custom-call(f32[8]{0:T(128)} %gain_ref.1, f32[4,2]{1,0:T(4,128)} %pad_maximum_fusion.coef_ref, bf16[16,256]{1,0:T(8,128)(2,1)} %fusion.2.emb_ref, bf16[2,128,2048]{2,1,0:T(8,128)(2,1)} %x_ref.1, bf16[128,2048]{1,0:T(8,128)(2,1)} %fresh_ref.1, bf16[256,3072]{1,0:T(8,128)(2,1)} %w_ref.1, ...), custom_call_target="tpu_custom_call" | custom-call | tf_op jit(solution)/shard_map/step/pallas_call | solution.py:609
  112.0 2.3 %copy.9 = bf16[2,128,2048]{2,1,0:T(8,128)(2,1)} copy(bf16[2,128,2048]{2,1,0:T(8,128)(2,1)} %step.1) | data formatting | bytes 2097152
  (2 shorter events, 0.0 us)

commit v6 on v5

--- a/solution.py
+++ b/solution.py
@@ -361,6 +361,11 @@
         for j in range(3):
             own_w(j, h).wait()
     fetch.wait()
+
+    @pl.when(f < 2)
+    def _():
+        past[2:] = jnp.zeros_like(past[2:])
+
     pl.semaphore_wait(barrier, len(partners))
 
     for g in range(2):
@@ -371,29 +376,34 @@
             emb_ref[...], w_mod_own[:, c : c + width // 2], preferred_element_type=jnp.float32
         )
 
-    def send_rows(i):
-        own = xg.at[side, pl.ds(i * rows, rows)]
-        return remote(own, own, xm_send.at[i], xm_recv.at[i], (f, at.s_side))
-
-    @pl.loop(0, frames * rows // 32)
-    def _(n):
-        per = rows // 32
-        i = n // per
-        spot = pl.ds(pl.multiple_of(lax.rem(n, per) * 32, 32), 32)
+    chunk = 32
+    chunks = frames * rows // chunk
+
+    def chunk_of(x, n):
+        return xg.at[x, pl.ds(pl.multiple_of(n * chunk, chunk), chunk)]
+
+    def send_rows(n):
+        own = chunk_of(side, n)
+        return remote(own, own, xm_send.at[n], xm_recv.at[n], (f, at.s_side))
+
+    def normalize(n):
+        i = n // (rows // chunk)
+        spot = pl.ds(pl.multiple_of(lax.rem(n, rows // chunk) * chunk, chunk), chunk)
         x32 = x_ref[i, spot, :].astype(jnp.float32)
         mean = jnp.mean(x32, axis=-1, keepdims=True)
         var = jnp.mean((x32 - mean) ** 2, axis=-1, keepdims=True)
         normed = (x32 - mean) * lax.rsqrt(var + 1e-06)
         xm = normed * (1.0 + mod[pl.ds(i, 1), width:]) + mod[pl.ds(i, 1), :width]
-        xg[side, pl.ds(pl.multiple_of(n * 32, 32), 32), :] = xm.astype(jnp.bfloat16)
-
-        for i in range(frames):
-            pl.when(n == (i + 1) * per - 1)(lambda: send_rows(i).start())
-
+        xg[side, pl.ds(pl.multiple_of(n * chunk, chunk), chunk), :] = xm.astype(jnp.bfloat16)
+        send_rows(n).start()
+
+    per_step = (chunks + at.pairs - 1) // at.pairs
+    pl.loop(0, per_step)(normalize)
     w_begin(0)
 
     @pl.loop(1, at.pairs)
     def _(k):
+        pl.loop(k * per_step, jnp.minimum((k + 1) * per_step, chunks))(normalize)
         w_step(0, k)
         pl.when(k == 1)(lambda: w_onward(1, s))
 
@@ -418,7 +428,7 @@
                 past[f, h, x, 1, i] = value_t
             pl.when(x == 0)(lambda: down(h).start())
             pl.when(x == 1)(lambda: up(h).start())
-            past_far(h, x).start()
+            pl.when(f < 2)(lambda: past_far(h, x).start())
             past_core(h, x).start()
             between(h)
 
@@ -445,14 +455,19 @@
     keys_values(side, q_steps)
     w_end(1)
     wo_steps(0)
-    for i in range(frames):
-        other = xg.at[1 - side, pl.ds(i * rows, rows)]
-        remote(other, other, xm_send.at[i], xm_recv.at[i], (f, at.s_side)).wait_recv()
+    @pl.loop(0, chunks)
+    def _(n):
+        other = chunk_of(1 - side, n)
+        remote(other, other, xm_send.at[n], xm_recv.at[n], (f, at.s_side)).wait_recv()
+
     keys_values(1 - side, lambda h: None)
     wo_steps(1)
     w_complete(1)
-    for h in range(heads):
-        past_pass(h, side)
+
+    @pl.when(f >= 2)
+    def _():
+        for h in range(heads):
+            past_pass(h, side)
 
     @pl.loop(0, heads // 2)
     def _(hp):
@@ -473,8 +488,7 @@
                     q_own[h, x, i] = query[i * rows : (i + 1) * rows].T.astype(jnp.bfloat16)
 
     wo_steps(2)
-    for i in range(frames):
-        send_rows(i).wait_send()
+    pl.loop(0, chunks)(lambda n: send_rows(n).wait_send())
     for g in range(2):
         w_finish(g)
 
@@ -486,12 +500,12 @@
 
     @pl.loop(0, heads)
     def _(h):
-        past_pass(h, 1 - side)
+        pl.when(f >= 2)(lambda: past_pass(h, 1 - side))
         down(h).wait_recv()
         up(h).wait_recv()
-        for g in (at.f_core, at.f_diag):
-            for x in range(2):
-                past_arrived(g, h, x)
+        for x in range(2):
+            past_arrived(at.f_core, h, x)
+            pl.when(f >= 2)(lambda: past_arrived(at.f_diag, h, x))
 
         @pl.loop(0, 2 * frames)
         def _(n):
@@ -538,8 +552,9 @@
         for copy in (down(h), up(h)):
             copy.wait_send()
         for x in range(2):
-            for copy in (past_far(h, x), past_core(h, x), past_passed(h, x)):
-                copy.wait_send()
+            past_core(h, x).wait_send()
+            pl.when(f < 2)(lambda: past_far(h, x).wait_send())
+            pl.when(f >= 2)(lambda: past_passed(h, x).wait_send())
 
     wo_complete()
     for h in range(heads):
@@ -625,7 +640,8 @@
             pltpu.VMEM(w_mod.shape, bf16),
             pltpu.VMEM((groups, rows, width // groups), bf16),
             pltpu.VMEM((groups, rows, width // groups), bf16),
-            dma((3, half)), dma((3,)), dma((groups,)), dma((frames,)), dma((frames,)),
+            dma((3, half)), dma((3,)), dma((groups,)),
+            dma((frames * rows // 32,)), dma((frames * rows // 32,)),
             dma((2,)), dma((2, space, 2)), dma((2, space)), dma((2, space)), dma((2, space)),
             dma((2, half, space)),
             dma((space, 2)), dma((space,)), dma((2, space)), dma((2, space)),

time: 115 us -> 115 us (level)
  no operation moved by 1% of the time
where the time goes in v6:
time: 115 us
  Pallas kernels  110 us (96%)
  other arithmetic  2.76 us (2%)
  local copies, waits for them, and re-layouts  2.3 us (2%)
    pallas_call x1, Pallas kernels, body(): pl.pallas_call(functools.partial(step_kernel, space), out_shape=jax.Shape...  110 us
    unnamed x1, local copies, waits for them, and re-layouts  2.3 us

profile of v6, /device:TPU:1, one launch (start us, length us, event | category | flops | bytes accessed | tf_op | source)
XLA Modules:
  0.0 115.0 jit_solution(6921550025527398990)
XLA Ops:
  0.0 0.7 convert_element_type.10
  0.7 0.1 fusion.3
  0.8 0.8 sqrt_bitcast_fusion.3
  1.6 0.6 pad_maximum_fusion.coef_ref
  2.2 0.6 fusion.2.emb_ref
  2.8 109.9 %step.1 = bf16[2,128,2048]{2,1,0:T(8,128)(2,1)} custom-call(f32[8]{0:T(128)} %gain_ref.1, f32[4,2]{1,0:T(4,128)} %pad_maximum_fusion.coef_ref, bf16[16,256]{1,0:T(8,128)(2,1)} %fusion.2.emb_ref, bf16[2,128,2048]{2,1,0:T(8,128)(2,1)} %x_ref.1, bf16[128,2048]{1,0:T(8,128)(2,1)} %fresh_ref.1, bf16[256,3072]{1,0:T(8,128)(2,1)} %w_ref.1, ...), custom_call_target="tpu_custom_call" | custom-call | tf_op jit(solution)/shard_map/step/pallas_call | solution.py:624
  112.7 2.3 %copy.9 = bf16[2,128,2048]{2,1,0:T(8,128)(2,1)} copy(bf16[2,128,2048]{2,1,0:T(8,128)(2,1)} %step.1) | data formatting | bytes 2097152
  (2 shorter events, 0.0 us)

commit v7 on v6

--- a/solution.py
+++ b/solution.py
@@ -238,8 +238,6 @@
     def wo_start():
         for way in (0, 1):
             at.onward(way, lambda to: wo_first(way, to).start())
-        for n in (0, 1):
-            wo_own_side(n).start()
         for c in range(cols):
             own_wo(c).start()
 
@@ -248,10 +246,17 @@
             wo_arrived(f, t)
             at.onward(way, lambda to: wo_next(t, way, to).start())
             wo_to_far(t).start()
-            wo_to_side(0, t).start()
             wo_to_core(0, t).start()
 
         at.at_distance(k, False, take)
+
+    def wo_over():
+        for n in (0, 1):
+            wo_own_side(n).start()
+
+        @pl.loop(1, at.pairs)
+        def _(k):
+            at.at_distance(k, False, lambda t, way: wo_to_side(0, t).start())
 
     def wo_pass_far(k):
         def take(t, way):
@@ -261,13 +266,15 @@
 
         at.at_distance(k, False, take)
 
-    def wo_pass_side():
-        @pl.loop(0, at.pairs)
-        def _(p):
+    def wo_pass_side(k):
+        def take(p):
             t = 2 * p + 1 - side
             for n in (0, 1):
                 wo_arrived((f, at.f_far)[n], t)
                 wo_to_core(n, t).start()
+
+        pl.when(at.pair >= k)(lambda: take(at.pair - k))
+        pl.when(jnp.logical_and(at.pair + k < at.pairs, k > 0))(lambda: take(at.pair + k))
 
     def wo_complete():
         def both(t):
@@ -438,14 +445,7 @@
         @pl.loop(h * stride + 1, jnp.minimum((h + 1) * stride, at.pairs - 1) + 1)
         def _(k):
             w_step(1, k)
-
-    wo_stride = (at.pairs - 1 + 2) // 3
-
-    def wo_steps(n):
-        for k in range(n * wo_stride + 1, min((n + 1) * wo_stride, at.pairs - 1) + 1):
             wo_spread(k)
-            if k >= 2:
-                wo_pass_far(k - 1)
 
     def past_pass(h, x):
         past_arrived(at.f_far, h, x)
@@ -454,14 +454,14 @@
     w_begin(1)
     keys_values(side, q_steps)
     w_end(1)
-    wo_steps(0)
     @pl.loop(0, chunks)
     def _(n):
         other = chunk_of(1 - side, n)
         remote(other, other, xm_send.at[n], xm_recv.at[n], (f, at.s_side)).wait_recv()
 
+    wo_over()
     keys_values(1 - side, lambda h: None)
-    wo_steps(1)
+    pl.loop(1, at.pairs)(wo_pass_far)
     w_complete(1)
 
     @pl.when(f >= 2)
@@ -487,7 +487,6 @@
                 for i in range(frames):
                     q_own[h, x, i] = query[i * rows : (i + 1) * rows].T.astype(jnp.bfloat16)
 
-    wo_steps(2)
     pl.loop(0, chunks)(lambda n: send_rows(n).wait_send())
     for g in range(2):
         w_finish(g)
@@ -542,10 +541,12 @@
 
         og[side, h] = o_own[side, h]
 
-        @pl.when(h == 0)
-        def _():
-            wo_pass_far(at.pairs - 1)
-            wo_pass_side()
+        last = at.pairs - 1
+        pl.loop(
+            jnp.clip((h - 1) * last // 2, 0, last), jnp.clip(h * last // 2, 0, last)
+        )(wo_pass_side)
+
+    wo_pass_side(at.pairs - 1)
 
     @pl.loop(0, heads)
     def _(h):

time: 115 us -> 106 us (0.922)
  Pallas kernels: 110 us -> 100 us
    pallas_call x1, Pallas kernels: 110 us -> 100 us  [body(): pl.pallas_call(functools.partial(step_kernel, space), out_shape=jax.Shape...]
where the time goes in v7:
time: 106 us; the launch traced here: 105 us
  Pallas kernels  100 us (94%)
  other arithmetic  2.76 us (3%)
  local copies, waits for them, and re-layouts  2.3 us (2%)
    pallas_call x1, Pallas kernels, body(): pl.pallas_call(functools.partial(step_kernel, space), out_shape=jax.Shape...  100 us
    unnamed x1, local copies, waits for them, and re-layouts  2.3 us

profile of v7, /device:TPU:1, one launch (start us, length us, event | category | flops | bytes accessed | tf_op | source)
XLA Modules:
  0.0 105.1 jit_solution(17754386063626629462)
XLA Ops:
  0.0 0.7 convert_element_type.10
  0.7 0.1 fusion.3
  0.8 0.8 sqrt_bitcast_fusion.3
  1.6 0.6 pad_maximum_fusion.coef_ref
  2.2 0.6 fusion.2.emb_ref
  2.8 100.0 %step.1 = bf16[2,128,2048]{2,1,0:T(8,128)(2,1)} custom-call(f32[8]{0:T(128)} %gain_ref.1, f32[4,2]{1,0:T(4,128)} %pad_maximum_fusion.coef_ref, bf16[16,256]{1,0:T(8,128)(2,1)} %fusion.2.emb_ref, bf16[2,128,2048]{2,1,0:T(8,128)(2,1)} %x_ref.1, bf16[128,2048]{1,0:T(8,128)(2,1)} %fresh_ref.1, bf16[256,3072]{1,0:T(8,128)(2,1)} %w_ref.1, ...), custom_call_target="tpu_custom_call" | custom-call | tf_op jit(solution)/shard_map/step/pallas_call | solution.py:625
  102.8 2.3 %copy.9 = bf16[2,128,2048]{2,1,0:T(8,128)(2,1)} copy(bf16[2,128,2048]{2,1,0:T(8,128)(2,1)} %step.1) | data formatting | bytes 2097152
  (2 shorter events, 0.0 us)

commit v8 on v7

--- a/solution.py
+++ b/solution.py
@@ -461,13 +461,7 @@
 
     wo_over()
     keys_values(1 - side, lambda h: None)
-    pl.loop(1, at.pairs)(wo_pass_far)
     w_complete(1)
-
-    @pl.when(f >= 2)
-    def _():
-        for h in range(heads):
-            past_pass(h, side)
 
     @pl.loop(0, heads // 2)
     def _(hp):
@@ -487,6 +481,13 @@
                 for i in range(frames):
                     q_own[h, x, i] = query[i * rows : (i + 1) * rows].T.astype(jnp.bfloat16)
 
+    @pl.when(f >= 2)
+    def _():
+        for h in range(heads):
+            past_pass(h, side)
+
+    pl.loop(1, at.pairs)(wo_pass_far)
+    pl.when(f >= 2)(lambda: past_pass(0, 1 - side))
     pl.loop(0, chunks)(lambda n: send_rows(n).wait_send())
     for g in range(2):
         w_finish(g)
@@ -499,7 +500,6 @@
 
     @pl.loop(0, heads)
     def _(h):
-        pl.when(f >= 2)(lambda: past_pass(h, 1 - side))
         down(h).wait_recv()
         up(h).wait_recv()
         for x in range(2):
@@ -533,11 +533,14 @@
             for g in range(groups * frames):
                 v_g = past[g // frames, h, b, 1, g % frames].astype(jnp.float32)
                 acc = acc + p_time[g : g + 1] * v_g
-            o_own[b, h, i, :, :] = (acc / total).T.astype(jnp.bfloat16)
+            o_own[b, h, i, :, :] = (acc * (1.0 / total)).T.astype(jnp.bfloat16)
 
             @pl.when(n == frames - 1)
             def _():
                 o_swap(h).start()
+                pl.when(jnp.logical_and(f >= 2, h + 1 < heads))(
+                    lambda: past_pass(h + 1, 1 - side)
+                )
 
         og[side, h] = o_own[side, h]
 
@@ -573,7 +576,7 @@
         for i in range(frames):
             x32 = x_ref[i, :, spot].astype(jnp.float32)
             eps = x32 + proj[i * rows : (i + 1) * rows]
-            clean = (x32 - coef_ref[0, i] * eps) / coef_ref[1, i]
+            clean = (x32 - coef_ref[0, i] * eps) * coef_ref[1, i]
             done = (coef_ref[2, i] * clean + coef_ref[3, i] * eps).astype(jnp.bfloat16)
             if i == 0:
                 leaving[c] = done
@@ -618,7 +621,7 @@
     a_now = alpha_bar(levels)
     a_later = alpha_bar(later)
     coefs = jnp.stack(
-        [jnp.sqrt(1.0 - a_now), jnp.sqrt(a_now), jnp.sqrt(a_later), jnp.sqrt(1.0 - a_later)]
+        [jnp.sqrt(1.0 - a_now), 1.0 / jnp.sqrt(a_now), jnp.sqrt(a_later), jnp.sqrt(1.0 - a_later)]
     )
     depth = w_qkv.shape[0]
     wo_depth = w_out.shape[0]

time: 106 us -> 106 us (level)
  no operation moved by 1% of the time
where the time goes in v8:
time: 106 us; the launch traced here: 105 us
  Pallas kernels  100 us (94%)
  other arithmetic  2.76 us (3%)
  local copies, waits for them, and re-layouts  2.3 us (2%)
    pallas_call x1, Pallas kernels, body(): pl.pallas_call(functools.partial(step_kernel, space), out_shape=jax.Shape...  100 us
    unnamed x1, local copies, waits for them, and re-layouts  2.3 us

profile of v8, /device:TPU:1, one launch (start us, length us, event | category | flops | bytes accessed | tf_op | source)
XLA Modules:
  0.0 105.1 jit_solution(1051115549286282278)
XLA Ops:
  0.0 0.7 convert_element_type.10
  0.7 0.1 fusion.3
  0.8 0.8 sqrt_bitcast_fusion.2
  1.6 0.6 pad_maximum_fusion.coef_ref
  2.2 0.6 fusion.2.emb_ref
  2.8 100.0 %step.1 = bf16[2,128,2048]{2,1,0:T(8,128)(2,1)} custom-call(f32[8]{0:T(128)} %gain_ref.1, f32[4,2]{1,0:T(4,128)} %pad_maximum_fusion.coef_ref, bf16[16,256]{1,0:T(8,128)(2,1)} %fusion.2.emb_ref, bf16[2,128,2048]{2,1,0:T(8,128)(2,1)} %x_ref.1, bf16[128,2048]{1,0:T(8,128)(2,1)} %fresh_ref.1, bf16[256,3072]{1,0:T(8,128)(2,1)} %w_ref.1, ...), custom_call_target="tpu_custom_call" | custom-call | tf_op jit(solution)/shard_map/step/pallas_call | solution.py:628
  102.8 2.3 %copy.9 = bf16[2,128,2048]{2,1,0:T(8,128)(2,1)} copy(bf16[2,128,2048]{2,1,0:T(8,128)(2,1)} %step.1) | data formatting | bytes 2097152
  (2 shorter events, 0.0 us)

commit v9 on v8

--- a/solution.py
+++ b/solution.py
@@ -404,7 +404,7 @@
         xg[side, pl.ds(pl.multiple_of(n * chunk, chunk), chunk), :] = xm.astype(jnp.bfloat16)
         send_rows(n).start()
 
-    per_step = (chunks + at.pairs - 1) // at.pairs
+    per_step = (chunks + 1) // 2
     pl.loop(0, per_step)(normalize)
     w_begin(0)
 

time: 106 us -> 106 us (level)
  no operation moved by 1% of the time
where the time goes in v9:
time: 106 us; the launch traced here: 105 us
  Pallas kernels  100 us (94%)
  other arithmetic  2.76 us (3%)
  local copies, waits for them, and re-layouts  2.3 us (2%)
    pallas_call x1, Pallas kernels, body(): pl.pallas_call(functools.partial(step_kernel, space), out_shape=jax.Shape...  100 us
    unnamed x1, local copies, waits for them, and re-layouts  2.3 us

profile of v9, /device:TPU:1, one launch (start us, length us, event | category | flops | bytes accessed | tf_op | source)
XLA Modules:
  0.0 105.1 jit_solution(8184801007547470513)
XLA Ops:
  0.0 0.7 convert_element_type.10
  0.7 0.1 fusion.3
  0.8 0.8 sqrt_bitcast_fusion.2
  1.6 0.6 pad_maximum_fusion.coef_ref
  2.2 0.6 fusion.2.emb_ref
  2.8 100.0 %step.1 = bf16[2,128,2048]{2,1,0:T(8,128)(2,1)} custom-call(f32[8]{0:T(128)} %gain_ref.1, f32[4,2]{1,0:T(4,128)} %pad_maximum_fusion.coef_ref, bf16[16,256]{1,0:T(8,128)(2,1)} %fusion.2.emb_ref, bf16[2,128,2048]{2,1,0:T(8,128)(2,1)} %x_ref.1, bf16[128,2048]{1,0:T(8,128)(2,1)} %fresh_ref.1, bf16[256,3072]{1,0:T(8,128)(2,1)} %w_ref.1, ...), custom_call_target="tpu_custom_call" | custom-call | tf_op jit(solution)/shard_map/step/pallas_call | solution.py:628
  102.8 2.3 %copy.9 = bf16[2,128,2048]{2,1,0:T(8,128)(2,1)} copy(bf16[2,128,2048]{2,1,0:T(8,128)(2,1)} %step.1) | data formatting | bytes 2097152
  (2 shorter events, 0.0 us)
